TPU v7x, 32 devices: a whole 2x2x4 slice. The times are simulated.
32 devices in a mesh: band: 4 (over y, x), tile: 4 (over z), slab: 2 (over core).
Axes of the slice: x: 2, y: 2, z: 4, core: 2. Of those that a mesh axis runs over, the one named last changes fastest.
Arguments:
- strength: float32 [32], P('band'), may hold values from 0.0005 to 0.5
- opacity: float32 [16, 64, 256], P('slab', 'tile'), may hold values from 0.5 to 2
- planck: float32 [16, 64, 256], P('slab', 'tile'), may hold values from 0.5 to 2
- old_populations: float32 [5, 16, 64, 256], P(None, 'slab', 'tile'), may hold values from 0.1 to 1
- line_index: int32 [32], P('band'), may hold values from 0 to 4
- line_weight: float32 [32], P('band'), may hold values from 0.2 to 1
Outputs:
- new_populations: float32 [5, 16, 64, 256], P(None, 'slab', 'tile', 'band')
- new_source: float32 [32, 16, 64, 256], P('band', 'slab', 'tile')
Inputs may be any that keep to these rules, and one draw needn't show every extreme that they name: line_index names a transition of the model atom.
All inputs are finite; a program needn't handle non-finite values.
Results may differ from a plain program's by a relative error of at most 0.0001.
Values sent between devices are 32-bit elements; how exact they have to be, the bound alone decides.
A program may use at most 64 MiB of HBM per device.

v0:
```python
import jax
import jax.numpy as jnp
from jax import lax
from jax.sharding import PartitionSpec as P

LINES = 5


EPS_THERMAL = 0.1
COLLISION = 0.5
PATH_FACTOR = 1.25
TILT_SHARE = 0.4
LOWER_LEVEL = (0, 0, 1, 1, 2)
UPPER_LEVEL = (3, 4, 3, 4, 4)


def extended_2(cells, sides, width):
    for axis, dim in sides:
        count = lax.axis_size(axis)
        ends = count - 1
        head = lax.slice_in_dim(cells, 0, width, axis=dim)
        tail = lax.slice_in_dim(cells, cells.shape[dim] - width, cells.shape[dim], axis=dim)
        cells = jnp.concatenate(
            [
                lax.ppermute(tail, axis, [(i, (i + 1) % count) for i in range(ends)]),
                cells,
                lax.ppermute(head, axis, [((i + 1) % count, i) for i in range(ends)]),
            ],
            axis=dim,
        )
    return cells


def shifted(block, axis, distance):
    devices = range(lax.axis_size(axis))
    route = [(i - distance, i) for i in devices if i - distance in devices]
    return lax.ppermute(block, axis, route)


def relax(jbar, planck):
    ratios = (jbar + COLLISION * planck[None]) / (1.0 + jbar + COLLISION)
    ground = jnp.ones_like(planck)
    level_three = ratios[0]
    level_four = ratios[1]
    level_one = 0.5 * (level_three / ratios[2] + level_four / ratios[3])
    level_two = level_four / ratios[4]
    stacked = jnp.stack([ground, level_one, level_two, level_three, level_four], axis=0)
    return stacked / jnp.sum(stacked, axis=0)


def line_sources(levels_now):
    return jnp.stack(
        [
            levels_now[UPPER_LEVEL[t]] / (levels_now[LOWER_LEVEL[t]] + levels_now[UPPER_LEVEL[t]])
            for t in range(5)
        ],
        axis=0,
    )


def sweep(face_ext, strength, opacity_ext, source_ext, margin):
    intensity = face_ext
    layer_sums = []
    for plane in range(opacity_ext.shape[0]):
        attenuation = jnp.exp(-PATH_FACTOR * strength[:, None, None] * opacity_ext[plane][None])[
            :, None
        ]
        zero_column = jnp.zeros_like(intensity[:, 0, :1])
        from_left = jnp.concatenate([zero_column, intensity[:, 0, :-1]], axis=1)
        from_right = jnp.concatenate([intensity[:, 1, 1:], zero_column], axis=1)
        upwind = jnp.stack([from_left, from_right], axis=1)
        intensity = (
            attenuation * ((1.0 - TILT_SHARE) * intensity + TILT_SHARE * upwind)
            + (1.0 - attenuation) * source_ext[:, plane][:, None]
        )
        layer_sums.append(jnp.sum(intensity[:, :, margin:-margin], axis=1))
    return (intensity[:, :, margin:-margin], jnp.stack(layer_sums, axis=1))


def per_device(strength, opacity, planck, old_populations, line_index, line_weight):
    highest = lax.Precision.HIGHEST
    slab_depth, tile_rows, cells_y = opacity.shape
    freq_count = strength.shape[0]
    total_freqs = freq_count * lax.axis_size("band")
    onehot = (line_index[:, None] == jnp.arange(LINES, dtype=jnp.int32)[None, :]).astype(
        jnp.float32
    )
    weighted = onehot * line_weight[:, None] * (LINES / (2.0 * total_freqs))
    fields = jnp.concatenate([opacity[None], planck[None], old_populations], axis=0)
    fields_ext = extended_2(fields, (("tile", 2),), slab_depth)
    opacity_ext = fields_ext[0]
    planck_ext = fields_ext[1]
    levels_ext = fields_ext[2:]
    extended = tile_rows + 2 * slab_depth
    global_x = (
        lax.axis_index("tile") * tile_rows - slab_depth + jnp.arange(extended, dtype=jnp.int32)
    )
    inside = ((global_x >= 0) & (global_x < tile_rows * lax.axis_size("tile")))[None, :, None]
    lower_ext = jnp.stack([levels_ext[LOWER_LEVEL[t]] for t in range(5)], axis=0)
    upper_ext = jnp.stack([levels_ext[UPPER_LEVEL[t]] for t in range(5)], axis=0)
    denominator = jnp.where(inside, lower_ext + upper_ext, 1.0)
    line_ext = jnp.where(inside, upper_ext / denominator, 0.0)
    source_ext = jnp.where(
        inside,
        EPS_THERMAL * planck_ext[None]
        + (1.0 - EPS_THERMAL) * jnp.einsum("ft,tzxy->fzxy", onehot, line_ext, precision=highest),
        0.0,
    )
    slab_count = lax.axis_size("slab")

    def whole_step(step, carry):
        face_in, previous = carry
        face_ext = extended_2(face_in, (("tile", 2),), slab_depth)
        bottom, layer_sums = sweep(face_ext, strength, opacity_ext, source_ext, slab_depth)
        return (shifted(bottom, "slab", 1), layer_sums)

    face_start = jnp.zeros((freq_count, 2, tile_rows, cells_y), jnp.float32)
    initial = (face_start, jnp.zeros((freq_count, slab_depth, tile_rows, cells_y), jnp.float32))
    _, layer_sums = lax.fori_loop(0, slab_count, whole_step, initial)
    jbar = jnp.einsum("ft,fzxy->tzxy", weighted, layer_sums, precision=highest)
    share = cells_y // lax.axis_size("band")
    offset = lax.axis_index("band") * share
    jbar_share = lax.psum_scatter(jbar, "band", scatter_dimension=3, tiled=True)
    planck_share = lax.dynamic_slice_in_dim(planck, offset, share, 2)
    populations_share = relax(jbar_share, planck_share)
    populations_all = lax.all_gather(populations_share, "band", axis=3, tiled=True)
    new_source = EPS_THERMAL * planck[None] + (1.0 - EPS_THERMAL) * jnp.einsum(
        "ft,tzxy->fzxy", onehot, line_sources(populations_all), precision=highest
    )
    return (populations_share, new_source)


def solution(mesh):
    in_specs = (
        P("band"),
        P("slab", "tile", None),
        P("slab", "tile", None),
        P(None, "slab", "tile", None),
        P("band"),
        P("band"),
    )
    out_specs = (P(None, "slab", "tile", "band"), P("band", "slab", "tile", None))
    return jax.shard_map(
        per_device, mesh=mesh, in_specs=in_specs, out_specs=out_specs, check_vma=False
    )
```

profile of v0, /device:TPU:1, one launch (start us, length us, event | category | flops | bytes accessed | tf_op | source)
XLA Modules:
  0.0 210.4 jit_solution(10125252328926001992)
XLA Ops:
  7.2 1.3 pad_maximum_fusion.3
  8.7 4.1 %collective-permute-start.3 = (f32[7,8,8,256]{3,2,1,0:T(8,128)S(1)}, f32[7,8,8,256]{3,2,1,0:T(8,128)S(1)}, u32[]{:S(2)}, u32[]{:S(2)}) collective-permute-start(f32[7,8,8,256]{3,2,1,0:T(8,128)S(1)} %get-tuple-element.112), channel_id=1, source_target_pairs={{0,2},{2,4},{4,6},{1,3},{3,5},{5,7},{8,10},{10,12},{12,14},{9,11},... | collective-permute-start | bytes 1376264 | tf_op jit(solution)/shard_map/ppermute | solution.py:25
  12.7 1.3 collective-permute-start.4
  14.1 7.8 %collective-permute-done.3 = f32[7,8,8,256]{3,2,1,0:T(8,128)S(1)} collective-permute-done((f32[7,8,8,256]{3,2,1,0:T(8,128)S(1)}, f32[7,8,8,256]{3,2,1,0:T(8,128)S(1)}, u32[]{:S(2)}, u32[]{:S(2)}) %collective-permute-start.3) | collective-permute-done | bytes 458784 | tf_op jit(solution)/shard_map/ppermute | solution.py:25
  22.6 3.2 %collective-permute-done.4 = f32[7,8,8,256]{3,2,1,0:T(8,128)} collective-permute-done((f32[7,8,8,256]{3,2,1,0:T(8,128)S(1)}, f32[7,8,8,256]{3,2,1,0:T(8,128)}, u32[]{:S(2)}, u32[]{:S(2)}) %collective-permute-start.4) | collective-permute-done | bytes 458784 | tf_op jit(solution)/shard_map/ppermute | solution.py:27
  25.8 1.3 pad_maximum_fusion.1
  28.1 1.8 fusion.27
  29.9 2.2 %fusion.26 = f32[8,8,32,256]{3,2,0,1:T(8,128)} fusion(f32[8,8,32,256]{3,0,2,1:T(8,128)S(1)} %fusion.27, f32[8,32,256]{2,1,0:T(8,128)S(1)} %get-tuple-element.105, pred[32]{0:T(512)(128)(4,1)S(1)} %compare_and_fusion), kind=kLoop, calls=%fused_computation.110 | loop fusion | flops 1572864 | bytes 4456480 | tf_op jit(solution)/shard_map/jit(_where)/select_n | solution.py:103
  32.2 50.5 %while.12 = (s32[]{:T(128)}, f32[8,2,16,256]{3,2,0,1:T(8,128)S(1)}, f32[8,8,16,256]{3,2,0,1:T(8,128)}, f32[8]{0:T(128)S(1)}, f32[8,32,256]{2,1,0:T(8,128)S(1)}, /*index=5*/f32[8,8,32,256]{3,2,0,1:T(8,128)}, s32[]{:T(128)}) while((s32[]{:T(128)}, f32[8,2,16,256]{3,2,0,1:T(8,128)S(1)}, f32[8,8,16,256]{3,2,0,1:T(8,128)}, f32[8]{0:T(128)S(1)}, ...), condition=%wide.region_9.10_spmd, body=%wide.region_0.9_spmd.sunk | while | flops 24772616 | bytes 81658408 | solution.py:119
  33.2 3.8 %collective-permute-start = (f32[8,2,8,256]{3,2,0,1:T(8,128)}, f32[8,2,8,256]{3,2,0,1:T(8,128)}, u32[]{:S(2)}, u32[]{:S(2)}) collective-permute-start(f32[8,2,8,256]{3,2,0,1:T(8,128)} %get-tuple-element.217), channel_id=1, source_target_pairs={{0,2},{2,4},{4,6},{1,3},{3,5},{5,7},{8,10},{10,12},{12,14},{9,11},... | collective-permute-start | bytes 393224 | tf_op jit(solution)/shard_map/while/body/eval_jaxpr/ppermute | solution.py:25
  37.0 1.3 collective-permute-start.1
  38.3 2.8 %multiply_bitcast_fusion.9 = (f32[8,32,256]{2,1,0:T(8,128)}, f32[8,32,256]{2,1,0:T(8,128)S(1)}, f32[8,32,256]{2,1,0:T(8,128)S(1)}, f32[8,32,256]{2,1,0:T(8,128)S...) fusion(f32[8,8,32,256]{3,2,0,1:T(8,128)} %get-tuple-element.274, ...), kind=kLoop, calls=%fused_computation.58.clone.1 | loop fusion | flops 1572864 | bytes 4456480 | tf_op jit(solution)/shard_map/while/body/eval_jaxpr/add | solution.py:73
  41.1 1.1 multiply_exponential_fusion.9
  42.9 0.9 constant_dynamic-update-slice_fusion.6
  43.8 1.0 constant_dynamic-update-slice_fusion.7
  44.8 0.9 constant_dynamic-update-slice_fusion.8
  48.5 0.8 copy-done
  49.3 0.8 fusion.75
  51.1 0.9 fusion.76
  52.2 0.8 copy-done.4
  53.0 1.3 collective-permute-start.2
  54.5 3.0 %collective-permute-done.2 = f32[8,2,16,256]{3,2,0,1:T(8,128)S(1)} collective-permute-done((f32[8,2,16,256]{3,2,0,1:T(8,128)S(1)}, f32[8,2,16,256]{3,2,0,1:T(8,128)S(1)}, u32[]{:S(2)}, u32[]{:S(2)}) %collective-permute-start.2) | collective-permute-done | bytes 262176 | tf_op jit(solution)/shard_map/while/body/eval_jaxpr/ppermute | solution.py:37
  58.3 4.9 %collective-permute-start = (f32[8,2,8,256]{3,2,0,1:T(8,128)}, f32[8,2,8,256]{3,2,0,1:T(8,128)}, u32[]{:S(2)}, u32[]{:S(2)}) collective-permute-start(f32[8,2,8,256]{3,2,0,1:T(8,128)} %get-tuple-element.217), channel_id=1, source_target_pairs={{0,2},{2,4},{4,6},{1,3},{3,5},{5,7},{8,10},{10,12},{12,14},{9,11},... | collective-permute-start | bytes 393224 | tf_op jit(solution)/shard_map/while/body/eval_jaxpr/ppermute | solution.py:25
  63.2 1.3 collective-permute-start.1
  64.5 2.8 %multiply_bitcast_fusion.9 = (f32[8,32,256]{2,1,0:T(8,128)}, f32[8,32,256]{2,1,0:T(8,128)S(1)}, f32[8,32,256]{2,1,0:T(8,128)S(1)}, f32[8,32,256]{2,1,0:T(8,128)S...) fusion(f32[8,8,32,256]{3,2,0,1:T(8,128)} %get-tuple-element.274, ...), kind=kLoop, calls=%fused_computation.58.clone.1 | loop fusion | flops 1572864 | bytes 4456480 | tf_op jit(solution)/shard_map/while/body/eval_jaxpr/add | solution.py:73
  67.3 1.1 multiply_exponential_fusion.9
  69.1 0.9 constant_dynamic-update-slice_fusion.6
  70.0 1.0 constant_dynamic-update-slice_fusion.7
  71.0 0.9 constant_dynamic-update-slice_fusion.8
  74.7 0.8 copy-done
  75.5 0.8 fusion.75
  77.3 0.9 fusion.76
  78.4 0.8 copy-done.4
  79.2 1.3 collective-permute-start.2
  80.7 2.0 collective-permute-done.2
  82.7 2.8 %fusion.33 = f32[5,8,16,256]{3,0,2,1:T(8,128)S(1)} fusion(f32[8,8,16,256]{3,2,0,1:T(8,128)} %get-tuple-element.33, f32[8]{0:T(128)S(1)} %copy-done.15, s32[8]{0:T(128)S(1)} %copy-done.14), kind=kOutput, calls=%fused_computation.121 | convolution fusion | flops 15728760 | bytes 1704000 | tf_op jit(solution)/shard_map/ft,fzxy->tzxy/dot_general | solution.py:120
  85.5 13.8 %copy.27 = f32[5,8,16,256]{0,2,1,3:T(8,128)} copy(f32[5,8,16,256]{3,0,2,1:T(8,128)S(1)} %fusion.33) | data formatting | bytes 1310720
  99.3 11.9 %reshape.106 = f32[256,640]{1,0:T(8,128)} reshape(f32[256,8,16,5]{3,2,1,0:T(8,128)} %bitcast.211) | data formatting | bytes 1310720
  112.0 24.7 %reduce-scatter.4.cloned.1.call-done = f32[64,640]{1,0:T(8,128)} async-done(((f32[256,640]{1,0:T(8,128)}), f32[64,640]{1,0:T(8,128)}) %reduce-scatter.4.cloned.1.call-update) | async-done | bytes 163856
  136.7 6.2 %reshape.107 = f32[64,8,16,5]{3,2,1,0:T(8,128)} reshape(f32[64,640]{1,0:T(8,128)} %reduce-scatter.4.cloned.1.call-done) | data formatting | bytes 327680
  142.9 3.8 %copy.28 = f32[5,8,16,64]{3,0,2,1:T(8,128)S(1)} copy(f32[5,8,16,64]{0,2,1,3:T(8,128)} %bitcast.212) | data formatting | bytes 327680
  148.2 0.8 copy.20
  149.0 45.4 %all_gather.3 = f32[5,8,16,256]{2,1,0,3:T(8,128)S(1)} all-gather(f32[5,8,16,64]{2,1,0,3:T(8,128)S(1)} %copy.14), channel_id=1, replica_groups=mesh['band'=4,'tile'=4,'slab'=2] {'band'}, dimensions={3}, use_global_device_ids=true | all-gather | bytes 819200 | tf_op jit(solution)/shard_map/all_gather | solution.py:126
  194.4 1.7 fusion.56
  196.1 1.5 copy.31
  197.6 1.5 copy.33
  200.5 1.1 stack.124
  202.2 1.3 copy.21
  (168 shorter events, 16.7 us)
Async XLA Ops:
  7.2 129.5 %reduce-scatter.4.cloned.1.call-start = ((), (), s32[]{:S(2)}) async-start(), calls=%async_computation.1 | async-start | bytes 819200
  7.2 18.6 %copy-start.7 = (f32[5,8,16,256]{3,2,1,0:T(8,128)S(1)}, f32[5,8,16,256]{3,2,1,0:T(8,128)}, u32[]{:S(2)}) copy-start(f32[5,8,16,256]{3,2,1,0:T(8,128)} %param.11) | copy-start | bytes 1966084
  7.2 18.6 %copy-start.8 = (f32[8,16,256]{2,1,0:T(8,128)S(1)}, f32[8,16,256]{2,1,0:T(8,128)}, u32[]{:S(2)}) copy-start(f32[8,16,256]{2,1,0:T(8,128)} %param.10) | copy-start | bytes 393220
  7.2 18.6 %copy-start.11 = (f32[8,16,256]{2,1,0:T(8,128)S(1)}, f32[8,16,256]{2,1,0:T(8,128)}, u32[]{:S(2)}) copy-start(f32[8,16,256]{2,1,0:T(8,128)} %param.9) | copy-start | bytes 393220
  8.7 13.2 %collective-permute-start.3 = (f32[7,8,8,256]{3,2,1,0:T(8,128)S(1)}, f32[7,8,8,256]{3,2,1,0:T(8,128)S(1)}, u32[]{:S(2)}, u32[]{:S(2)}) collective-permute-start(f32[7,8,8,256]{3,2,1,0:T(8,128)S(1)} %get-tuple-element.112), channel_id=1, source_target_pairs={{0,2},{2,4},{4,6},{1,3},{3,5},{5,7},{8,10},{10,12},{12,14},{9,11},... | collective-permute-start | bytes 1376264 | tf_op jit(solution)/shard_map/ppermute | solution.py:25
  12.7 13.1 %collective-permute-start.4 = (f32[7,8,8,256]{3,2,1,0:T(8,128)S(1)}, f32[7,8,8,256]{3,2,1,0:T(8,128)}, u32[]{:S(2)}, u32[]{:S(2)}) collective-permute-start(f32[7,8,8,256]{3,2,1,0:T(8,128)S(1)} %get-tuple-element.113), channel_id=1, source_target_pairs={{2,0},{4,2},{6,4},{3,1},{5,3},{7,5},{10,8},{12,10},{14,12},{11,9},... | collective-permute-start | bytes 1376264 | tf_op jit(solution)/shard_map/ppermute | solution.py:27
  21.9 0.8 copy-start.13
  27.4 0.7 copy-start.14
  29.9 2.2 %copy-start.16 = (f32[8]{0:T(128)S(1)}, f32[8]{0:T(128)}, u32[]{:S(2)}) copy-start(f32[8]{0:T(128)} %param.8) | copy-start | bytes 100
  32.2 50.5 %copy-start.15 = (f32[8]{0:T(128)S(1)}, f32[8]{0:T(128)}, u32[]{:S(2)}) copy-start(f32[8]{0:T(128)} %param.13) | copy-start | bytes 100
  32.4 5.9 %copy-start.1 = (f32[8,2,16,256]{3,2,0,1:T(8,128)}, f32[8,2,16,256]{3,2,0,1:T(8,128)S(1)}, u32[]{:S(2)}) copy-start(f32[8,2,16,256]{3,2,0,1:T(8,128)S(1)} %get-tuple-element.263) | copy-start | bytes 786436 | tf_op jit(solution)/shard_map/while
  32.4 5.9 %copy-start.5 = (f32[8,32,256]{2,1,0:T(8,128)}, f32[8,32,256]{2,1,0:T(8,128)S(1)}, u32[]{:S(2)}) copy-start(f32[8,32,256]{2,1,0:T(8,128)S(1)} %get-tuple-element.273) | copy-start | bytes 786436 | tf_op jit(solution)/shard_map/while
  33.2 9.7 %collective-permute-start = (f32[8,2,8,256]{3,2,0,1:T(8,128)}, f32[8,2,8,256]{3,2,0,1:T(8,128)}, u32[]{:S(2)}, u32[]{:S(2)}) collective-permute-start(f32[8,2,8,256]{3,2,0,1:T(8,128)} %get-tuple-element.217), channel_id=1, source_target_pairs={{0,2},{2,4},{4,6},{1,3},{3,5},{5,7},{8,10},{10,12},{12,14},{9,11},... | collective-permute-start | bytes 393224 | tf_op jit(solution)/shard_map/while/body/eval_jaxpr/ppermute | solution.py:25
  37.0 7.8 %collective-permute-start.1 = (f32[8,2,8,256]{3,2,0,1:T(8,128)}, f32[8,2,8,256]{3,2,0,1:T(8,128)}, u32[]{:S(2)}, u32[]{:S(2)}) collective-permute-start(f32[8,2,8,256]{3,2,0,1:T(8,128)} %get-tuple-element.218), channel_id=1, source_target_pairs={{2,0},{4,2},{6,4},{3,1},{5,3},{7,5},{10,8},{12,10},{14,12},{11,9},... | collective-permute-start | bytes 393224 | tf_op jit(solution)/shard_map/while/body/eval_jaxpr/ppermute | solution.py:27
  48.4 1.0 copy-start
  50.1 1.0 copy-start.2
  50.1 1.0 copy-start.3
  52.1 0.9 copy-start.4
  53.0 4.5 %copy-start.6 = (f32[8,32,256]{2,1,0:T(8,128)S(1)}, f32[8,32,256]{2,1,0:T(8,128)}, u32[]{:S(2)}) copy-start(f32[8,32,256]{2,1,0:T(8,128)} %copy-done.5) | copy-start | bytes 786436 | tf_op jit(solution)/shard_map/while
  53.0 4.4 %collective-permute-start.2 = (f32[8,2,16,256]{3,2,0,1:T(8,128)S(1)}, f32[8,2,16,256]{3,2,0,1:T(8,128)S(1)}, u32[]{:S(2)}, u32[]{:S(2)}) collective-permute-start(f32[8,2,16,256]{3,2,0,1:T(8,128)S(1)} %get-tuple-element.252), channel_id=1, source_target_pairs={{0,1},{2,3},{4,5},{6,7},{8,9},{10,11},{12,13},{14,15},{16,17},{18,... | collective-permute-start | bytes 786440 | tf_op jit(solution)/shard_map/while/body/eval_jaxpr/ppermute | solution.py:37
  54.5 3.0 %copy-start.10 = (f32[8,8,16,256]{3,2,0,1:T(8,128)}, f32[8,8,16,256]{3,2,0,1:T(8,128)S(1)}, u32[]{:S(2)}) copy-start(f32[8,8,16,256]{3,2,0,1:T(8,128)S(1)} %bitcast_dynamic-update-slice_fusion.23) | copy-start | bytes 3145732 | tf_op jit(solution)/shard_map/while
  57.5 7.0 %copy-start.1 = (f32[8,2,16,256]{3,2,0,1:T(8,128)}, f32[8,2,16,256]{3,2,0,1:T(8,128)S(1)}, u32[]{:S(2)}) copy-start(f32[8,2,16,256]{3,2,0,1:T(8,128)S(1)} %get-tuple-element.263) | copy-start | bytes 786436 | tf_op jit(solution)/shard_map/while
  57.5 7.0 %copy-start.5 = (f32[8,32,256]{2,1,0:T(8,128)}, f32[8,32,256]{2,1,0:T(8,128)S(1)}, u32[]{:S(2)}) copy-start(f32[8,32,256]{2,1,0:T(8,128)S(1)} %get-tuple-element.273) | copy-start | bytes 786436 | tf_op jit(solution)/shard_map/while
  58.3 10.8 %collective-permute-start = (f32[8,2,8,256]{3,2,0,1:T(8,128)}, f32[8,2,8,256]{3,2,0,1:T(8,128)}, u32[]{:S(2)}, u32[]{:S(2)}) collective-permute-start(f32[8,2,8,256]{3,2,0,1:T(8,128)} %get-tuple-element.217), channel_id=1, source_target_pairs={{0,2},{2,4},{4,6},{1,3},{3,5},{5,7},{8,10},{10,12},{12,14},{9,11},... | collective-permute-start | bytes 393224 | tf_op jit(solution)/shard_map/while/body/eval_jaxpr/ppermute | solution.py:25
  63.2 7.8 %collective-permute-start.1 = (f32[8,2,8,256]{3,2,0,1:T(8,128)}, f32[8,2,8,256]{3,2,0,1:T(8,128)}, u32[]{:S(2)}, u32[]{:S(2)}) collective-permute-start(f32[8,2,8,256]{3,2,0,1:T(8,128)} %get-tuple-element.218), channel_id=1, source_target_pairs={{2,0},{4,2},{6,4},{3,1},{5,3},{7,5},{10,8},{12,10},{14,12},{11,9},... | collective-permute-start | bytes 393224 | tf_op jit(solution)/shard_map/while/body/eval_jaxpr/ppermute | solution.py:27
  74.6 1.0 copy-start
  76.3 1.0 copy-start.2
  76.3 1.0 copy-start.3
  78.3 0.9 copy-start.4
  79.2 3.5 %copy-start.6 = (f32[8,32,256]{2,1,0:T(8,128)S(1)}, f32[8,32,256]{2,1,0:T(8,128)}, u32[]{:S(2)}) copy-start(f32[8,32,256]{2,1,0:T(8,128)} %copy-done.5) | copy-start | bytes 786436 | tf_op jit(solution)/shard_map/while
  79.2 3.4 %collective-permute-start.2 = (f32[8,2,16,256]{3,2,0,1:T(8,128)S(1)}, f32[8,2,16,256]{3,2,0,1:T(8,128)S(1)}, u32[]{:S(2)}, u32[]{:S(2)}) collective-permute-start(f32[8,2,16,256]{3,2,0,1:T(8,128)S(1)} %get-tuple-element.252), channel_id=1, source_target_pairs={{0,1},{2,3},{4,5},{6,7},{8,9},{10,11},{12,13},{14,15},{16,17},{18,... | collective-permute-start | bytes 786440 | tf_op jit(solution)/shard_map/while/body/eval_jaxpr/ppermute | solution.py:37
  80.7 2.0 copy-start.10
  99.3 11.9 %copy-start.9 = (f32[8,16,256]{2,1,0:T(8,128)S(1)}, f32[8,16,256]{2,1,0:T(8,128)}, u32[]{:S(2)}) copy-start(f32[8,16,256]{2,1,0:T(8,128)} %param.10) | copy-start | bytes 393220
  200.0 1.6 copy-start.12
Sparse Core Ops, SparseCore 0:
  111.3 25.3 reduce-scatter.3
where the time goes:
time: 214 us; the launch traced here: 210 us
  local copies, waits for them, and re-layouts  61.6 us (29%)
  blocking collectives  45.4 us (21%)
  waiting for transfers between devices  40.7 us (19%)
  other arithmetic  22.7 us (11%)
  starting transfers between devices  19.2 us (9%)
  between operations  14.3 us (7%)
  matrix products  5.26 us (2%)
    all_gather x1, blocking collectives, per_device(): lax.all_gather(populations_share, 'band', axis=3, tiled=True)  45.4 us
    unnamed x29, local copies, waits for them, and re-layouts  43.1 us
    unnamed x2, waiting for transfers between devices  24.7 us
    add x16, other arithmetic, sweep(): attenuation * ((1.0 - TILT_SHARE) * intensity + TILT_SHARE * upwind)  12.8 us
    ppermute x3, starting transfers between devices, extended_2(): lax.ppermute(tail, axis, [(i, (i + 1) % count) for i in range(ends)])  12.8 us
    while x50, local copies, waits for them, and re-layouts  8.85 us
    ppermute x3, waiting for transfers between devices, extended_2(): lax.ppermute(tail, axis, [(i, (i + 1) % count) for i in range(ends)])  7.81 us
    ppermute x2, waiting for transfers between devices, shifted(): return lax.ppermute(block, axis, route)  4.98 us
  transfers between devices with their start and end apart: 9, of which 5 were waited for; matrix products, arithmetic and copies ran while one was open for 7% of the time, Pallas kernels for 0%

commit v1 on v0

v1 whole, which is shorter than its diff:
```python
import functools

import jax
import jax.numpy as jnp
from jax import lax
from jax.experimental import pallas as pl
from jax.experimental.pallas import tpu as pltpu
from jax.sharding import PartitionSpec as P

MESH = pl.DeviceIdType.MESH
LINES = 5
LEVELS = 5
EPS_THERMAL = 0.1
COLLISION = 0.5
PATH_FACTOR = 1.25
TILT_SHARE = 0.4
LOWER_LEVEL = (0, 0, 1, 1, 2)
UPPER_LEVEL = (3, 4, 3, 4, 4)
LANES = 128
ROWS = 8
HALF = LANES // 2
BATCH = 4


def half_turn(v):
    return pltpu.roll(v, HALF, 1)


def kernel(
    sizes,
    strength,
    line_index,
    line_weight,
    opacity,
    planck,
    populations,
    pops_out,
    source_out,
    fields,
    planck_all,
    par_f,
    par_i,
    par_s,
    halo_out,
    halo_in,
    opac,
    src,
    plk,
    face_in,
    face_halo,
    face_out,
    acc,
    gathered,
    new_src,
    in_sem,
    idx_sem,
    par_send,
    par_recv,
    halo_send,
    halo_recv,
    face_send,
    face_recv,
    gat_send,
    gat_recv,
):
    bands, tiles, slabs, depth, freqs = sizes
    pairs = depth // 2
    subs = freqs // BATCH
    band = lax.axis_index("band")
    tile = lax.axis_index("tile")
    slab = lax.axis_index("slab")
    has_left = tile > 0
    has_right = tile < tiles - 1
    has_up = slab > 0
    has_down = slab < slabs - 1

    column = pl.multiple_of((band // 2) * LANES, LANES)
    loads = [
        pltpu.make_async_copy(opacity.at[:, :, pl.ds(column, LANES)], fields.at[0], in_sem.at[0]),
        pltpu.make_async_copy(planck.at[:, :, pl.ds(column, LANES)], fields.at[1], in_sem.at[1]),
        pltpu.make_async_copy(
            populations.at[:, :, :, pl.ds(column, LANES)], fields.at[pl.ds(2, LEVELS)], in_sem.at[2]
        ),
        pltpu.make_async_copy(planck, planck_all, in_sem.at[3]),
    ]
    for load in loads:
        load.start()

    barrier = pltpu.get_barrier_semaphore()
    for k in range(1, bands):
        pl.semaphore_signal(
            barrier, inc=1, device_id={"band": lax.rem(band + k, bands)}, device_id_type=MESH
        )
    expected = jnp.int32(bands - 1)
    for dt in (-1, 0, 1):
        for ds in (-1, 0, 1):
            if dt == 0 and ds == 0:
                continue
            there = (tile + dt >= 0) & (tile + dt < tiles) & (slab + ds >= 0) & (slab + ds < slabs)

            @pl.when(there)
            def _():
                pl.semaphore_signal(
                    barrier,
                    inc=1,
                    device_id={"tile": tile + dt, "slab": slab + ds},
                    device_id_type=MESH,
                )

            expected = expected + there.astype(jnp.int32)

    row = lax.broadcasted_iota(jnp.int32, (ROWS, LANES), 0)
    lane = lax.broadcasted_iota(jnp.int32, (ROWS, LANES), 1)
    left = lane < HALF
    own = (lane // HALF) == lax.rem(band, 2)
    top_left = left & (row == 0)
    low_right = jnp.logical_not(left) & (row == ROWS - 1)

    lane_row = lax.broadcasted_iota(jnp.int32, (1, LANES), 1)
    indices = jnp.zeros((1, LANES), jnp.int32)
    zero = jnp.zeros((ROWS, LANES), jnp.float32)
    rate, weight, which = zero, zero, zero
    for f in range(freqs):
        here = row == f
        rate = jnp.where(here, -PATH_FACTOR * strength[f], rate)
        weight = jnp.where(here, line_weight[f] * (LINES / (2.0 * freqs * bands)), weight)
        which = jnp.where(here, line_index[f].astype(jnp.float32), which)
        indices = jnp.where(lane_row == f, line_index[f], indices)
    par_f[0, 0] = rate
    par_f[0, 1] = weight
    par_f[0, 2] = which
    par_i[0] = indices

    @pl.when(jnp.logical_not(has_left))
    def _():
        halo_in[0] = jnp.zeros(halo_in.shape[1:], jnp.float32)
        face_halo[0] = jnp.zeros(face_halo.shape[1:], jnp.float32)

    @pl.when(jnp.logical_not(has_right))
    def _():
        halo_in[1] = jnp.zeros(halo_in.shape[1:], jnp.float32)
        face_halo[1] = jnp.zeros(face_halo.shape[1:], jnp.float32)

    @pl.when(jnp.logical_not(has_up))
    def _():
        face_in[...] = jnp.zeros(face_in.shape, jnp.float32)
        face_halo[...] = jnp.zeros(face_halo.shape, jnp.float32)

    acc[...] = jnp.zeros(acc.shape, jnp.float32)

    pl.semaphore_wait(barrier, expected)

    def par_copies(k):
        to = {"band": lax.rem(band + k, bands)}
        return (
            pltpu.make_async_remote_copy(
                src_ref=par_f.at[0],
                dst_ref=par_f.at[k],
                send_sem=par_send.at[0, k],
                recv_sem=par_recv.at[0, k],
                device_id=to,
                device_id_type=MESH,
            ),
            pltpu.make_async_remote_copy(
                src_ref=par_i.at[0],
                dst_ref=par_i.at[k],
                send_sem=par_send.at[1, k],
                recv_sem=par_recv.at[1, k],
                device_id=to,
                device_id_type=MESH,
            ),
        )

    for k in range(1, bands):
        for copy in par_copies(k):
            copy.start()

    for load in loads[:3]:
        load.wait()

    def spread(v):
        return jnp.where(own, v, half_turn(v))

    def prepare(zp, carry):
        packs = [[], []]
        for z in (zp, zp + pairs):
            for half in range(2):
                rows = pl.ds(half * ROWS, ROWS)
                o = spread(fields[0, z, rows])
                p = spread(fields[1, z, rows])
                levels = [spread(fields[2 + i, z, rows]) for i in range(LEVELS)]
                opac[z, half] = o
                plk[z, half] = p
                values = [o]
                for t in range(LINES):
                    low, up = levels[LOWER_LEVEL[t]], levels[UPPER_LEVEL[t]]
                    s = EPS_THERMAL * p + (1.0 - EPS_THERMAL) * (up / (low + up))
                    src[t, z, half] = s
                    values.append(s)
                packs[half].append(values)
        for i in range(1 + LINES):
            halo_out[0, zp, i] = jnp.where(left, packs[1][0][i], packs[1][1][i])
            halo_out[1, zp, i] = jnp.where(left, packs[0][1][i], packs[0][0][i])
        return carry

    lax.fori_loop(0, pairs, prepare, 0)

    def halo_copy(side):
        return pltpu.make_async_remote_copy(
            src_ref=halo_out.at[side],
            dst_ref=halo_in.at[side],
            send_sem=halo_send.at[side],
            recv_sem=halo_recv.at[side],
            device_id={"tile": tile + (1 if side == 0 else -1)},
            device_id_type=MESH,
        )

    @pl.when(has_right)
    def _():
        halo_copy(0).start()

    @pl.when(has_left)
    def _():
        halo_copy(1).start()

    for k in range(1, bands):
        for copy in par_copies(k):
            copy.wait_recv()
    to_scalars = pltpu.make_async_copy(par_i, par_s, idx_sem)
    to_scalars.start()
    to_scalars.wait()

    @pl.when(has_left)
    def _():
        halo_copy(0).wait_recv()

    @pl.when(has_right)
    def _():
        halo_copy(1).wait_recv()

    def unpack(zp, carry):
        for i in range(1 + LINES):
            a, b = halo_in[0, zp, i], halo_in[1, zp, i]
            first = jnp.where(left, a, b)
            second = half_turn(jnp.where(left, b, a))
            if i == 0:
                opac[zp, 2] = first
                opac[zp + pairs, 2] = second
            else:
                src[i - 1, zp, 2] = first
                src[i - 1, zp + pairs, 2] = second
        return carry

    lax.fori_loop(0, pairs, unpack, 0)

    def face_copies(chunk):
        def make(part, source, target, to):
            return pltpu.make_async_remote_copy(
                src_ref=source,
                dst_ref=target,
                send_sem=face_send.at[part, chunk],
                recv_sem=face_recv.at[part, chunk],
                device_id=to,
                device_id_type=MESH,
            )

        return (
            make(0, face_out.at[chunk], face_in.at[chunk], {"slab": slab + 1}),
            make(
                1,
                face_out.at[chunk, 1],
                face_halo.at[0, chunk],
                {"tile": tile + 1, "slab": slab + 1},
            ),
            make(
                2,
                face_out.at[chunk, 0],
                face_halo.at[1, chunk],
                {"tile": tile - 1, "slab": slab + 1},
            ),
        )

    def chunk_step(k, sub):
        chunk = k * subs + sub
        main, to_right, to_left = face_copies(chunk)

        @pl.when(has_up)
        def _():
            main.wait_recv()

        @pl.when(has_up & has_left)
        def _():
            to_right.wait_recv()

        @pl.when(has_up & has_right)
        def _():
            to_left.wait_recv()

        states, rates, weights, indices = [], [], [], []
        for f in range(BATCH):
            at = pl.ds(sub * BATCH + f, 1)
            rates.append(jnp.broadcast_to(par_f[k, 0, at], (ROWS, LANES)))
            w = jnp.broadcast_to(par_f[k, 1, at], (ROWS, LANES))
            t_of = jnp.broadcast_to(par_f[k, 2, at], (ROWS, LANES))
            weights.append([jnp.where(t_of == float(t), w, 0.0) for t in range(LINES)])
            indices.append(par_s[k, 0, sub * BATCH + f])
            beyond = jnp.where(left, face_halo[0, chunk, f], face_halo[1, chunk, f])
            states.append((face_in[chunk, 0, f], face_in[chunk, 1, f], beyond))
        for z in range(depth):
            last = z == depth - 1
            o = [opac[z, i] for i in range(2 if last else 3)]
            for f in range(BATCH):
                one, two, out = states[f]
                d1, d2, dh = (pltpu.roll(v, 1, 0) for v in (one, two, out))
                u1, u2, uh = (pltpu.roll(v, ROWS - 1, 0) for v in (one, two, out))
                winds = [
                    jnp.where(top_left, dh, jnp.where(low_right, u2, jnp.where(left, d1, u1))),
                    jnp.where(top_left, d1, jnp.where(low_right, uh, jnp.where(left, d2, u2))),
                    jnp.where(left, dh, uh),
                ]
                fresh = []
                for i in range(len(o)):
                    s = src[indices[f], z, i]
                    a = jnp.exp(rates[f] * o[i])
                    mixed = (1.0 - TILT_SHARE) * states[f][i] + TILT_SHARE * winds[i]
                    fresh.append(s + a * (mixed - s))
                if last:
                    fresh.append(out)
                states[f] = tuple(fresh)
            for half in range(2):
                for t in range(LINES):
                    total = acc[t, z, half]
                    for f in range(BATCH):
                        total = total + weights[f][t] * states[f][half]
                    acc[t, z, half] = total
        for f in range(BATCH):
            face_out[chunk, 0, f] = states[f][0]
            face_out[chunk, 1, f] = states[f][1]

        @pl.when(has_down)
        def _():
            main.start()

        @pl.when(has_down & has_right)
        def _():
            to_right.start()

        @pl.when(has_down & has_left)
        def _():
            to_left.start()

    def group_step(k, carry):
        for sub in range(subs):
            chunk_step(k, sub)
        return carry

    lax.fori_loop(0, bands, group_step, 0)

    def gather_copy(k, zp):
        return pltpu.make_async_remote_copy(
            src_ref=gathered.at[band, zp],
            dst_ref=gathered.at[band, zp],
            send_sem=gat_send.at[k, zp],
            recv_sem=gat_recv.at[k, zp],
            device_id={"band": lax.rem(band + k, bands)},
            device_id_type=MESH,
        )

    def arrival(k, zp):
        sender = lax.rem(band + bands - k, bands)
        return pltpu.make_async_remote_copy(
            src_ref=gathered.at[sender, zp],
            dst_ref=gathered.at[sender, zp],
            send_sem=gat_send.at[k, zp],
            recv_sem=gat_recv.at[k, zp],
            device_id={"band": lax.rem(band + k, bands)},
            device_id_type=MESH,
        )

    def relax(zp, carry):
        for half in range(2):
            both = []
            for z in (zp, zp + pairs):
                p = COLLISION * plk[z, half]
                ratios = []
                for t in range(LINES):
                    j = acc[t, z, half]
                    j = j + half_turn(j)
                    ratios.append((j + p) / ((1.0 + COLLISION) + j))
                one = 0.5 * (ratios[0] / ratios[2] + ratios[1] / ratios[3])
                levels = (one, ratios[1] / ratios[4], ratios[0], ratios[1])
                both.append(levels)
                scale = 1.0 / (1.0 + levels[0] + levels[1] + levels[2] + levels[3])
                rows = pl.ds(half * ROWS, ROWS)
                pops_out[0, z, rows] = scale[:, :HALF]
                for i in range(4):
                    pops_out[1 + i, z, rows] = (scale * levels[i])[:, :HALF]
            for i in range(4):
                gathered[band, zp, i, half] = jnp.where(left, both[0][i], both[1][i])
        for k in range(1, bands):
            gather_copy(k, zp).start()
        return carry

    lax.fori_loop(0, pairs, relax, 0)

    loads[3].wait()

    def finish(zp, carry):
        for k in range(1, bands):
            arrival(k, zp).wait_recv()
        for pair in range(bands // 2):
            columns = slice(pair * LANES, (pair + 1) * LANES)
            for half in range(2):
                rows = pl.ds(half * ROWS, ROWS)
                lines = []
                for b in (2 * pair, 2 * pair + 1):
                    levels = [1.0] + [gathered[b, zp, i, half] for i in range(4)]
                    lines.append(
                        [
                            levels[UPPER_LEVEL[t]] / (levels[LOWER_LEVEL[t]] + levels[UPPER_LEVEL[t]])
                            for t in range(LINES)
                        ]
                    )
                first = EPS_THERMAL * planck_all[zp, rows, columns]
                second = EPS_THERMAL * planck_all[zp + pairs, rows, columns]
                for t in range(LINES):
                    even, odd = lines[0][t], lines[1][t]
                    new_src[t, zp, rows, columns] = first + (1.0 - EPS_THERMAL) * jnp.where(
                        left, even, half_turn(odd)
                    )
                    new_src[t, zp + pairs, rows, columns] = second + (
                        1.0 - EPS_THERMAL
                    ) * jnp.where(left, half_turn(even), odd)
        for f in range(freqs):
            t = line_index[f]
            source_out[f, zp] = new_src[t, zp]
            source_out[f, zp + pairs] = new_src[t, zp + pairs]
        return carry

    lax.fori_loop(0, pairs, finish, 0)

    for k in range(1, bands):
        for copy in par_copies(k):
            copy.wait_send()

    @pl.when(has_right)
    def _():
        halo_copy(0).wait_send()

    @pl.when(has_left)
    def _():
        halo_copy(1).wait_send()

    def drain(chunk, carry):
        main, to_right, to_left = face_copies(chunk)

        @pl.when(has_down)
        def _():
            main.wait_send()

        @pl.when(has_down & has_right)
        def _():
            to_right.wait_send()

        @pl.when(has_down & has_left)
        def _():
            to_left.wait_send()

        return carry

    lax.fori_loop(0, bands * subs, drain, 0)

    def drain_gather(zp, carry):
        for k in range(1, bands):
            gather_copy(k, zp).wait_send()
        return carry

    lax.fori_loop(0, pairs, drain_gather, 0)


def per_device(sizes, strength, opacity, planck, old_populations, line_index, line_weight):
    bands, tiles, slabs = sizes
    depth, rows, cells = opacity.shape
    freqs = strength.shape[0]
    pairs = depth // 2
    chunks = bands * freqs // BATCH
    assert rows == 2 * ROWS and depth <= ROWS and cells == bands * HALF
    f32 = jnp.float32
    scalars = pl.BlockSpec(memory_space=pltpu.SMEM)
    anywhere = pl.BlockSpec(memory_space=pl.ANY)
    vmem = pl.BlockSpec(memory_space=pltpu.VMEM)
    sem = pltpu.SemaphoreType.DMA
    tile = (ROWS, LANES)
    return pl.pallas_call(
        functools.partial(kernel, (bands, tiles, slabs, depth, freqs)),
        out_shape=(
            jax.ShapeDtypeStruct((LEVELS, depth, rows, cells // bands), f32),
            jax.ShapeDtypeStruct((freqs, depth, rows, cells), f32),
        ),
        in_specs=[scalars] * 3 + [anywhere] * 3,
        out_specs=(vmem, vmem),
        scratch_shapes=[
            pltpu.VMEM((2 + LEVELS, depth, rows, LANES), f32),
            pltpu.VMEM((depth, rows, cells), f32),
            pltpu.VMEM((bands, 3) + tile, f32),
            pltpu.VMEM((bands, 1, LANES), jnp.int32),
            pltpu.SMEM((bands, 1, LANES), jnp.int32),
            pltpu.VMEM((2, pairs, 1 + LINES) + tile, f32),
            pltpu.VMEM((2, pairs, 1 + LINES) + tile, f32),
            pltpu.VMEM((depth, 3) + tile, f32),
            pltpu.VMEM((LINES, depth, 3) + tile, f32),
            pltpu.VMEM((depth, 2) + tile, f32),
            pltpu.VMEM((chunks, 2, BATCH) + tile, f32),
            pltpu.VMEM((2, chunks, BATCH) + tile, f32),
            pltpu.VMEM((chunks, 2, BATCH) + tile, f32),
            pltpu.VMEM((LINES, depth, 2) + tile, f32),
            pltpu.VMEM((bands, pairs, 4, 2) + tile, f32),
            pltpu.VMEM((LINES, depth, rows, cells), f32),
            sem((4,)),
            sem,
            sem((2, bands)),
            sem((2, bands)),
            sem((2,)),
            sem((2,)),
            sem((3, chunks)),
            sem((3, chunks)),
            sem((bands, pairs)),
            sem((bands, pairs)),
        ],
        compiler_params=pltpu.CompilerParams(
            collective_id=0, has_side_effects=True, vmem_limit_bytes=32 * 1024 * 1024
        ),
        cost_estimate=pl.CostEstimate(
            flops=60 * depth * rows * cells * freqs,
            bytes_accessed=16 * depth * rows * cells * 4,
            transcendentals=2 * depth * rows * cells * freqs,
        ),
    )(strength, line_index, line_weight, opacity, planck, old_populations)


def solution(mesh):
    sizes = (mesh.shape["band"], mesh.shape["tile"], mesh.shape["slab"])
    in_specs = (
        P("band"),
        P("slab", "tile", None),
        P("slab", "tile", None),
        P(None, "slab", "tile", None),
        P("band"),
        P("band"),
    )
    out_specs = (P(None, "slab", "tile", "band"), P("band", "slab", "tile", None))
    return jax.shard_map(
        functools.partial(per_device, sizes),
        mesh=mesh,
        in_specs=in_specs,
        out_specs=out_specs,
        check_vma=False,
    )
```

time: 214 us -> 29.2 us (0.14); the launches traced: 210 us -> 29 us
  local copies, waits for them, and re-layouts: 61.6 us -> 6.55 us
  blocking collectives: 45.4 us -> 0 us
  waiting for transfers between devices: 40.7 us -> 0 us
  other arithmetic: 22.7 us -> 0 us
  Pallas kernels: 0 us -> 21.8 us
  starting transfers between devices: 19.2 us -> 0 us
  between operations: 14.3 us -> 0.65 us
  matrix products: 5.26 us -> 0 us
    all_gather x1 -> x0, blocking collectives: 45.4 us -> none  [per_device(): lax.all_gather(populations_share, 'band', axis=3, tiled=True)]
    unnamed x29 -> x14, local copies, waits for them, and re-layouts: 43.1 us -> 6.55 us
    unnamed x2 -> x0, waiting for transfers between devices: 24.7 us -> none
    pallas_call x0 -> x1, Pallas kernels: none -> 21.8 us  [per_device(): pl.pallas_call(functools.partial(kernel, (bands, tiles, slabs, depth, fre...]
    ppermute x8 -> x0, starting transfers between devices: 19.2 us -> none  [the longest x3 12.8 us: extended_2(): lax.ppermute(tail, axis, [(i, (i + 1) % count) for i in range(ends)])]
    ppermute x8 -> x0, waiting for transfers between devices: 16 us -> none  [the longest x3 7.81 us: extended_2(): lax.ppermute(tail, axis, [(i, (i + 1) % count) for i in range(ends)])]
    add x17 -> x0, other arithmetic: 12.9 us -> none  [the longest x16 12.8 us: sweep(): attenuation * ((1.0 - TILT_SHARE) * intensity + TILT_SHARE * upwind)]
    while x50 -> x0, local copies, waits for them, and re-layouts: 8.85 us -> none
  transfers between devices with their start and end apart: 9 -> 0, of which waited for: 5 -> 0; matrix products, arithmetic and copies ran while one was open for 7% -> 0% of each run, Pallas kernels for 0% -> 0%
where the time goes in v1:
time: 29.2 us; the launch traced here: 29 us
  Pallas kernels  21.8 us (75%)
  local copies, waits for them, and re-layouts  6.55 us (22%)
  between operations  0.65 us (2%)
    pallas_call x1, Pallas kernels, per_device(): pl.pallas_call(functools.partial(kernel, (bands, tiles, slabs, depth, fre...  21.8 us
    unnamed x14, local copies, waits for them, and re-layouts  6.55 us

profile of v1, /device:TPU:1, one launch (start us, length us, event | category | flops | bytes accessed | tf_op | source)
XLA Modules:
  0.0 29.0 jit_solution(16391366333469039256)
XLA Ops:
  0.6 0.0 copy-start
  0.6 1.1 %copy-done = f32[5,8,16,256]{3,2,1,0:T(8,128)S(1)} copy-done((f32[5,8,16,256]{3,2,1,0:T(8,128)S(1)}, f32[5,8,16,256]{3,2,1,0:T(8,128)}, u32[]{:S(2)}) %copy-start) | copy-done | bytes 655384
  1.7 0.0 copy-start.1
  1.7 0.9 %copy-done.1 = f32[8,16,256]{2,1,0:T(8,128)S(1)} copy-done((f32[8,16,256]{2,1,0:T(8,128)S(1)}, f32[8,16,256]{2,1,0:T(8,128)}, u32[]{:S(2)}) %copy-start.1) | copy-done | bytes 131096
  2.6 0.0 copy-start.2
  2.6 0.9 %copy-done.2 = f32[8,16,256]{2,1,0:T(8,128)S(1)} copy-done((f32[8,16,256]{2,1,0:T(8,128)S(1)}, f32[8,16,256]{2,1,0:T(8,128)}, u32[]{:S(2)}) %copy-start.2) | copy-done | bytes 131096
  3.5 0.0 copy-start.3
  3.5 0.7 %copy-done.3 = f32[8]{0:T(128)S(1)} copy-done((f32[8]{0:T(128)S(1)}, f32[8]{0:T(128)}, u32[]{:S(2)}) %copy-start.3) | copy-done | bytes 56
  4.2 0.0 copy-start.4
  4.2 0.7 %copy-done.4 = s32[8]{0:T(128)S(1)} copy-done((s32[8]{0:T(128)S(1)}, s32[8]{0:T(128)}, u32[]{:S(2)}) %copy-start.4) | copy-done | bytes 56
  4.8 0.0 copy-start.5
  4.8 0.7 %copy-done.5 = f32[8]{0:T(128)S(1)} copy-done((f32[8]{0:T(128)S(1)}, f32[8]{0:T(128)}, u32[]{:S(2)}) %copy-start.5) | copy-done | bytes 56
  5.5 21.8 %shard_map.77 = (f32[5,8,16,64]{3,2,1,0:T(8,128)S(1)}, f32[8,8,16,256]{3,2,1,0:T(8,128)S(1)}) custom-call(f32[8]{0:T(128)S(1)} %copy-done.3, s32[8]{0:T(128)S(1)} %copy-done.4, f32[8]{0:T(128)S(1)} %copy-done.5, f32[8,16,256]{2,1,0:T(8,128)S(1)} %copy-done.1, f32[8,16,256]{2,1,0:T(8,128)S(1)} %copy-done.2, f32[5,8,16,256]{3,2,1,0:T(8,128)S(1)} %copy-done), custom_call_target="tpu_custom_call" | custom-call | flops 15728640 | bytes 2097152 | tf_op jit(solution)/shard_map/pallas_call | solution.py:494
  27.3 0.7 %copy.10 = f32[5,8,16,64]{3,2,1,0:T(8,128)} copy(f32[5,8,16,64]{3,2,1,0:T(8,128)S(1)} %get-tuple-element.4) | data formatting | bytes 327680
  28.0 1.0 %copy.11 = f32[8,8,16,256]{3,2,1,0:T(8,128)} copy(f32[8,8,16,256]{3,2,1,0:T(8,128)S(1)} %get-tuple-element.5) | data formatting | bytes 2097152
Async XLA Ops:
  0.6 1.1 %copy-start = (f32[5,8,16,256]{3,2,1,0:T(8,128)S(1)}, f32[5,8,16,256]{3,2,1,0:T(8,128)}, u32[]{:S(2)}) copy-start(f32[5,8,16,256]{3,2,1,0:T(8,128)} %populations.1) | copy-start | bytes 1966084
  1.7 0.9 %copy-start.1 = (f32[8,16,256]{2,1,0:T(8,128)S(1)}, f32[8,16,256]{2,1,0:T(8,128)}, u32[]{:S(2)}) copy-start(f32[8,16,256]{2,1,0:T(8,128)} %opacity.1) | copy-start | bytes 393220
  2.6 0.9 %copy-start.2 = (f32[8,16,256]{2,1,0:T(8,128)S(1)}, f32[8,16,256]{2,1,0:T(8,128)}, u32[]{:S(2)}) copy-start(f32[8,16,256]{2,1,0:T(8,128)} %planck.1) | copy-start | bytes 393220
  3.5 0.7 %copy-start.3 = (f32[8]{0:T(128)S(1)}, f32[8]{0:T(128)}, u32[]{:S(2)}) copy-start(f32[8]{0:T(128)} %strength.1) | copy-start | bytes 100
  4.2 0.7 %copy-start.4 = (s32[8]{0:T(128)S(1)}, s32[8]{0:T(128)}, u32[]{:S(2)}) copy-start(s32[8]{0:T(128)} %line_index.1) | copy-start | bytes 100
  4.8 0.7 %copy-start.5 = (f32[8]{0:T(128)S(1)}, f32[8]{0:T(128)}, u32[]{:S(2)}) copy-start(f32[8]{0:T(128)} %line_weight.1) | copy-start | bytes 100

commit v2 on v1

--- a/solution.py
+++ b/solution.py
@@ -28,14 +28,17 @@
 
 def kernel(
     sizes,
-    strength,
-    line_index,
-    line_weight,
+    strength_hbm,
+    line_index_hbm,
+    line_weight_hbm,
     opacity,
     planck,
     populations,
     pops_out,
     source_out,
+    strength,
+    line_index,
+    line_weight,
     fields,
     planck_all,
     par_f,
@@ -81,7 +84,10 @@
         pltpu.make_async_copy(
             populations.at[:, :, :, pl.ds(column, LANES)], fields.at[pl.ds(2, LEVELS)], in_sem.at[2]
         ),
-        pltpu.make_async_copy(planck, planck_all, in_sem.at[3]),
+        pltpu.make_async_copy(strength_hbm, strength, in_sem.at[3]),
+        pltpu.make_async_copy(line_index_hbm, line_index, in_sem.at[4]),
+        pltpu.make_async_copy(line_weight_hbm, line_weight, in_sem.at[5]),
+        pltpu.make_async_copy(planck, planck_all, in_sem.at[6]),
     ]
     for load in loads:
         load.start()
@@ -116,21 +122,6 @@
     top_left = left & (row == 0)
     low_right = jnp.logical_not(left) & (row == ROWS - 1)
 
-    lane_row = lax.broadcasted_iota(jnp.int32, (1, LANES), 1)
-    indices = jnp.zeros((1, LANES), jnp.int32)
-    zero = jnp.zeros((ROWS, LANES), jnp.float32)
-    rate, weight, which = zero, zero, zero
-    for f in range(freqs):
-        here = row == f
-        rate = jnp.where(here, -PATH_FACTOR * strength[f], rate)
-        weight = jnp.where(here, line_weight[f] * (LINES / (2.0 * freqs * bands)), weight)
-        which = jnp.where(here, line_index[f].astype(jnp.float32), which)
-        indices = jnp.where(lane_row == f, line_index[f], indices)
-    par_f[0, 0] = rate
-    par_f[0, 1] = weight
-    par_f[0, 2] = which
-    par_i[0] = indices
-
     @pl.when(jnp.logical_not(has_left))
     def _():
         halo_in[0] = jnp.zeros(halo_in.shape[1:], jnp.float32)
@@ -147,8 +138,6 @@
         face_halo[...] = jnp.zeros(face_halo.shape, jnp.float32)
 
     acc[...] = jnp.zeros(acc.shape, jnp.float32)
-
-    pl.semaphore_wait(barrier, expected)
 
     def par_copies(k):
         to = {"band": lax.rem(band + k, bands)}
@@ -171,39 +160,62 @@
             ),
         )
 
+    for load in loads[:6]:
+        load.wait()
+
+    lane_row = lax.broadcasted_iota(jnp.int32, (1, LANES), 1)
+    indices = jnp.zeros((1, LANES), jnp.int32)
+    zero = jnp.zeros((ROWS, LANES), jnp.float32)
+    rate, weight, which = zero, zero, zero
+    for f in range(freqs):
+        here = row == f
+        rate = jnp.where(here, -PATH_FACTOR * strength[f], rate)
+        weight = jnp.where(here, line_weight[f] * (LINES / (2.0 * freqs * bands)), weight)
+        which = jnp.where(here, line_index[f].astype(jnp.float32), which)
+        indices = jnp.where(lane_row == f, line_index[f], indices)
+    par_f[0, 0] = rate
+    par_f[0, 1] = weight
+    par_f[0, 2] = which
+    par_i[0] = indices
+
+    def spread(v):
+        return jnp.where(own, v, half_turn(v))
+
+    def prepare(z, carry):
+        for half in range(2):
+            rows = pl.ds(half * ROWS, ROWS)
+            p = spread(fields[1, z, rows])
+            levels = [spread(fields[2 + i, z, rows]) for i in range(LEVELS)]
+            opac[z, half] = spread(fields[0, z, rows])
+            plk[z, half] = p
+            for t in range(LINES):
+                low, up = levels[LOWER_LEVEL[t]], levels[UPPER_LEVEL[t]]
+                src[t, z, half] = EPS_THERMAL * p + (1.0 - EPS_THERMAL) * (up / (low + up))
+        return carry
+
+    lax.fori_loop(0, depth, prepare, 0)
+
+    def layer(i, z, part):
+        return opac[z, part] if i == 0 else src[i - 1, z, part]
+
+    for i in range(1 + LINES):
+        right, down = [], []
+        for z in range(pairs):
+            y = depth - 2 - z
+            a, b = layer(i, z, 1), layer(i, z, 0)
+            if y > z:
+                a = jnp.where(row >= 1 + z, a, pltpu.roll(layer(i, y, 1), z + 1, 0))
+                b = jnp.where(row <= y, b, pltpu.roll(layer(i, y, 0), y + 1, 0))
+            right.append(a)
+            down.append(b)
+        for q in range(pairs // 2):
+            halo_out[0, i, q] = jnp.where(left, right[q], right[q + pairs // 2])
+            halo_out[1, i, q] = jnp.where(left, down[q + pairs // 2], down[q])
+
+    pl.semaphore_wait(barrier, expected)
     for k in range(1, bands):
         for copy in par_copies(k):
             copy.start()
-
-    for load in loads[:3]:
-        load.wait()
-
-    def spread(v):
-        return jnp.where(own, v, half_turn(v))
-
-    def prepare(zp, carry):
-        packs = [[], []]
-        for z in (zp, zp + pairs):
-            for half in range(2):
-                rows = pl.ds(half * ROWS, ROWS)
-                o = spread(fields[0, z, rows])
-                p = spread(fields[1, z, rows])
-                levels = [spread(fields[2 + i, z, rows]) for i in range(LEVELS)]
-                opac[z, half] = o
-                plk[z, half] = p
-                values = [o]
-                for t in range(LINES):
-                    low, up = levels[LOWER_LEVEL[t]], levels[UPPER_LEVEL[t]]
-                    s = EPS_THERMAL * p + (1.0 - EPS_THERMAL) * (up / (low + up))
-                    src[t, z, half] = s
-                    values.append(s)
-                packs[half].append(values)
-        for i in range(1 + LINES):
-            halo_out[0, zp, i] = jnp.where(left, packs[1][0][i], packs[1][1][i])
-            halo_out[1, zp, i] = jnp.where(left, packs[0][1][i], packs[0][0][i])
-        return carry
-
-    lax.fori_loop(0, pairs, prepare, 0)
 
     def halo_copy(side):
         return pltpu.make_async_remote_copy(
@@ -238,20 +250,22 @@
     def _():
         halo_copy(1).wait_recv()
 
-    def unpack(zp, carry):
-        for i in range(1 + LINES):
-            a, b = halo_in[0, zp, i], halo_in[1, zp, i]
-            first = jnp.where(left, a, b)
-            second = half_turn(jnp.where(left, b, a))
-            if i == 0:
-                opac[zp, 2] = first
-                opac[zp + pairs, 2] = second
-            else:
-                src[i - 1, zp, 2] = first
-                src[i - 1, zp + pairs, 2] = second
-        return carry
-
-    lax.fori_loop(0, pairs, unpack, 0)
+    for i in range(1 + LINES):
+        for q in range(pairs // 2):
+            a, b = halo_in[0, i, q], halo_in[1, i, q]
+            shared = {q: jnp.where(left, a, b)}
+            shared[q + pairs // 2] = half_turn(jnp.where(left, b, a))
+            for z, tile_rows in shared.items():
+                y = depth - 2 - z
+                both = [(z, tile_rows)]
+                if y > z:
+                    moved = (pltpu.roll(tile_rows, y + 1, 0), pltpu.roll(tile_rows, z + 1, 0))
+                    both.append((y, jnp.where(left, *moved)))
+                for at, v in both:
+                    if i == 0:
+                        opac[at, 2] = v
+                    else:
+                        src[i - 1, at, 2] = v
 
     def face_copies(chunk):
         def make(part, source, target, to):
@@ -356,24 +370,17 @@
 
     lax.fori_loop(0, bands, group_step, 0)
 
-    def gather_copy(k, zp):
+    beside = band + 1 - 2 * lax.rem(band, 2)
+    across = lax.rem(band + 2, bands)
+    corner = bands - 1 - band
+
+    def gather_copy(kind, owner, zp, to):
         return pltpu.make_async_remote_copy(
-            src_ref=gathered.at[band, zp],
-            dst_ref=gathered.at[band, zp],
-            send_sem=gat_send.at[k, zp],
-            recv_sem=gat_recv.at[k, zp],
-            device_id={"band": lax.rem(band + k, bands)},
-            device_id_type=MESH,
-        )
-
-    def arrival(k, zp):
-        sender = lax.rem(band + bands - k, bands)
-        return pltpu.make_async_remote_copy(
-            src_ref=gathered.at[sender, zp],
-            dst_ref=gathered.at[sender, zp],
-            send_sem=gat_send.at[k, zp],
-            recv_sem=gat_recv.at[k, zp],
-            device_id={"band": lax.rem(band + k, bands)},
+            src_ref=gathered.at[owner, zp],
+            dst_ref=gathered.at[owner, zp],
+            send_sem=gat_send.at[kind, zp],
+            recv_sem=gat_recv.at[kind, zp],
+            device_id={"band": to},
             device_id_type=MESH,
         )
 
@@ -397,17 +404,33 @@
                     pops_out[1 + i, z, rows] = (scale * levels[i])[:, :HALF]
             for i in range(4):
                 gathered[band, zp, i, half] = jnp.where(left, both[0][i], both[1][i])
-        for k in range(1, bands):
-            gather_copy(k, zp).start()
+        gather_copy(0, band, zp, beside).start()
+        gather_copy(1, band, zp, across).start()
         return carry
 
     lax.fori_loop(0, pairs, relax, 0)
 
-    loads[3].wait()
-
-    def finish(zp, carry):
-        for k in range(1, bands):
-            arrival(k, zp).wait_recv()
+    loads[6].wait()
+
+    def forward(q, carry):
+        gather_copy(0, beside, 2 * q, beside).wait_recv()
+        gather_copy(2, beside, 2 * q, across).start()
+        gather_copy(1, across, 2 * q + 1, across).wait_recv()
+        gather_copy(2, across, 2 * q + 1, beside).start()
+        return carry
+
+    lax.fori_loop(0, pairs // 2, forward, 0)
+
+    def finish_two(q, carry):
+        gather_copy(1, across, 2 * q, across).wait_recv()
+        gather_copy(2, corner, 2 * q, corner).wait_recv()
+        finish(2 * q)
+        gather_copy(0, beside, 2 * q + 1, beside).wait_recv()
+        gather_copy(2, corner, 2 * q + 1, corner).wait_recv()
+        finish(2 * q + 1)
+        return carry
+
+    def finish(zp):
         for pair in range(bands // 2):
             columns = slice(pair * LANES, (pair + 1) * LANES)
             for half in range(2):
@@ -435,9 +458,8 @@
             t = line_index[f]
             source_out[f, zp] = new_src[t, zp]
             source_out[f, zp + pairs] = new_src[t, zp + pairs]
-        return carry
-
-    lax.fori_loop(0, pairs, finish, 0)
+
+    lax.fori_loop(0, pairs // 2, finish_two, 0)
 
     for k in range(1, bands):
         for copy in par_copies(k):
@@ -471,11 +493,22 @@
     lax.fori_loop(0, bands * subs, drain, 0)
 
     def drain_gather(zp, carry):
-        for k in range(1, bands):
-            gather_copy(k, zp).wait_send()
+        gather_copy(0, band, zp, beside).wait_send()
+        gather_copy(1, band, zp, across).wait_send()
+        gather_copy(2, corner, zp, across).wait_send()
         return carry
 
     lax.fori_loop(0, pairs, drain_gather, 0)
+
+
+def write_out(pops, source, pops_hbm, source_hbm, sem):
+    copies = [pltpu.make_async_copy(pops, pops_hbm, sem.at[0])]
+    for f in range(source.shape[0]):
+        copies.append(pltpu.make_async_copy(source.at[f], source_hbm.at[f], sem.at[1 + f]))
+    for copy in copies:
+        copy.start()
+    for copy in copies:
+        copy.wait()
 
 
 def per_device(sizes, strength, opacity, planck, old_populations, line_index, line_weight):
@@ -484,29 +517,32 @@
     freqs = strength.shape[0]
     pairs = depth // 2
     chunks = bands * freqs // BATCH
-    assert rows == 2 * ROWS and depth <= ROWS and cells == bands * HALF
+    assert rows == 2 * ROWS and depth == ROWS and cells == bands * HALF and bands == 4
     f32 = jnp.float32
-    scalars = pl.BlockSpec(memory_space=pltpu.SMEM)
+    hbm = pl.BlockSpec(memory_space=pltpu.HBM)
     anywhere = pl.BlockSpec(memory_space=pl.ANY)
     vmem = pl.BlockSpec(memory_space=pltpu.VMEM)
     sem = pltpu.SemaphoreType.DMA
     tile = (ROWS, LANES)
-    return pl.pallas_call(
+    pops, source = pl.pallas_call(
         functools.partial(kernel, (bands, tiles, slabs, depth, freqs)),
         out_shape=(
             jax.ShapeDtypeStruct((LEVELS, depth, rows, cells // bands), f32),
             jax.ShapeDtypeStruct((freqs, depth, rows, cells), f32),
         ),
-        in_specs=[scalars] * 3 + [anywhere] * 3,
+        in_specs=[hbm] * 6,
         out_specs=(vmem, vmem),
         scratch_shapes=[
+            pltpu.SMEM((freqs,), f32),
+            pltpu.SMEM((freqs,), jnp.int32),
+            pltpu.SMEM((freqs,), f32),
             pltpu.VMEM((2 + LEVELS, depth, rows, LANES), f32),
             pltpu.VMEM((depth, rows, cells), f32),
             pltpu.VMEM((bands, 3) + tile, f32),
             pltpu.VMEM((bands, 1, LANES), jnp.int32),
             pltpu.SMEM((bands, 1, LANES), jnp.int32),
-            pltpu.VMEM((2, pairs, 1 + LINES) + tile, f32),
-            pltpu.VMEM((2, pairs, 1 + LINES) + tile, f32),
+            pltpu.VMEM((2, 1 + LINES, pairs // 2) + tile, f32),
+            pltpu.VMEM((2, 1 + LINES, pairs // 2) + tile, f32),
             pltpu.VMEM((depth, 3) + tile, f32),
             pltpu.VMEM((LINES, depth, 3) + tile, f32),
             pltpu.VMEM((depth, 2) + tile, f32),
@@ -516,7 +552,7 @@
             pltpu.VMEM((LINES, depth, 2) + tile, f32),
             pltpu.VMEM((bands, pairs, 4, 2) + tile, f32),
             pltpu.VMEM((LINES, depth, rows, cells), f32),
-            sem((4,)),
+            sem((7,)),
             sem,
             sem((2, bands)),
             sem((2, bands)),
@@ -524,8 +560,8 @@
             sem((2,)),
             sem((3, chunks)),
             sem((3, chunks)),
-            sem((bands, pairs)),
-            sem((bands, pairs)),
+            sem((3, pairs)),
+            sem((3, pairs)),
         ],
         compiler_params=pltpu.CompilerParams(
             collective_id=0, has_side_effects=True, vmem_limit_bytes=32 * 1024 * 1024
@@ -535,7 +571,22 @@
             bytes_accessed=16 * depth * rows * cells * 4,
             transcendentals=2 * depth * rows * cells * freqs,
         ),
-    )(strength, line_index, line_weight, opacity, planck, old_populations)
+    )(
+        *(
+            pltpu.with_memory_space_constraint(v, pltpu.HBM)
+            for v in (strength, line_index, line_weight, opacity, planck, old_populations)
+        )
+    )
+    return pl.pallas_call(
+        write_out,
+        out_shape=(
+            jax.ShapeDtypeStruct(pops.shape, f32),
+            jax.ShapeDtypeStruct(source.shape, f32),
+        ),
+        in_specs=[anywhere] * 2,
+        out_specs=(hbm, hbm),
+        scratch_shapes=[sem((1 + freqs,))],
+    )(pops, source)
 
 
 def solution(mesh):

time: 29.2 us -> 65.9 us (2.26)
  Pallas kernels: 21.8 us -> 63.4 us
  local copies, waits for them, and re-layouts: 6.55 us -> 1.69 us
    pallas_call x0 -> x1, Pallas kernels: none -> 42.9 us  [per_device(): pl.pallas_call(write_out, out_shape=(jax.ShapeDtypeStruct(pops.shape, f32...]
    unnamed x14 -> x4, local copies, waits for them, and re-layouts: 6.55 us -> 1.69 us
    pallas_call x1, Pallas kernels: 21.8 us -> 20.5 us  [per_device(): pl.pallas_call(functools.partial(kernel, (bands, tiles, slabs, depth, fre...]
where the time goes in v2:
time: 65.9 us; the launch traced here: 65.8 us
  Pallas kernels  63.4 us (96%)
  local copies, waits for them, and re-layouts  1.69 us (3%)
    pallas_call x1, Pallas kernels, per_device(): pl.pallas_call(write_out, out_shape=(jax.ShapeDtypeStruct(pops.shape, f32...  42.9 us
    pallas_call x1, Pallas kernels, per_device(): pl.pallas_call(functools.partial(kernel, (bands, tiles, slabs, depth, fre...  20.5 us
    unnamed x4, local copies, waits for them, and re-layouts  1.69 us

profile of v2, /device:TPU:1, one launch (start us, length us, event | category | flops | bytes accessed | tf_op | source)
XLA Modules:
  0.0 65.8 jit_solution(3972132675990703515)
XLA Ops:
  0.6 20.5 %shard_map.77 = (f32[5,8,16,64]{3,2,1,0:T(8,128)S(1)}, f32[8,8,16,256]{3,2,1,0:T(8,128)S(1)}) custom-call(f32[8]{0:T(128)} %strength_hbm.1, s32[8]{0:T(128)} %line_index_hbm.1, f32[8]{0:T(128)} %line_weight_hbm.1, f32[8,16,256]{2,1,0:T(8,128)} %opacity.1, f32[8,16,256]{2,1,0:T(8,128)} %planck.1, f32[5,8,16,256]{3,2,1,0:T(8,128)} %populations.1), custom_call_target="tpu_custom_call" | custom-call | flops 15728640 | bytes 2097152 | tf_op jit(solution)/shard_map/pallas_call | solution.py:527
  21.2 0.0 copy-start
  21.2 1.0 %copy-done = f32[8,8,16,256]{3,2,1,0:T(8,128)} copy-done((f32[8,8,16,256]{3,2,1,0:T(8,128)}, f32[8,8,16,256]{3,2,1,0:T(8,128)S(1)}, u32[]{:S(2)}) %copy-start) | copy-done | bytes 1048600
  22.2 0.0 copy-start.1
  22.2 0.7 %copy-done.1 = f32[5,8,16,64]{3,2,1,0:T(8,128)} copy-done((f32[5,8,16,64]{3,2,1,0:T(8,128)}, f32[5,8,16,64]{3,2,1,0:T(8,128)S(1)}, u32[]{:S(2)}) %copy-start.1) | copy-done | bytes 163864
  22.9 42.9 %shard_map.78 = (f32[5,8,16,64]{3,2,1,0:T(8,128)}, f32[8,8,16,256]{3,2,1,0:T(8,128)}) custom-call(f32[5,8,16,64]{3,2,1,0:T(8,128)} %copy-done.1, f32[8,8,16,256]{3,2,1,0:T(8,128)} %copy-done), custom_call_target="tpu_custom_call" | custom-call | tf_op jit(solution)/shard_map/pallas_call | solution.py:580
Async XLA Ops:
  21.2 1.0 %copy-start = (f32[8,8,16,256]{3,2,1,0:T(8,128)}, f32[8,8,16,256]{3,2,1,0:T(8,128)S(1)}, u32[]{:S(2)}) copy-start(f32[8,8,16,256]{3,2,1,0:T(8,128)S(1)} %get-tuple-element.5.source) | copy-start | bytes 3145732
  22.2 0.7 %copy-start.1 = (f32[5,8,16,64]{3,2,1,0:T(8,128)}, f32[5,8,16,64]{3,2,1,0:T(8,128)S(1)}, u32[]{:S(2)}) copy-start(f32[5,8,16,64]{3,2,1,0:T(8,128)S(1)} %get-tuple-element.4.pops) | copy-start | bytes 491524

commit v3 on v2

--- a/solution.py
+++ b/solution.py
@@ -520,7 +520,6 @@
     assert rows == 2 * ROWS and depth == ROWS and cells == bands * HALF and bands == 4
     f32 = jnp.float32
     hbm = pl.BlockSpec(memory_space=pltpu.HBM)
-    anywhere = pl.BlockSpec(memory_space=pl.ANY)
     vmem = pl.BlockSpec(memory_space=pltpu.VMEM)
     sem = pltpu.SemaphoreType.DMA
     tile = (ROWS, LANES)
@@ -583,10 +582,13 @@
             jax.ShapeDtypeStruct(pops.shape, f32),
             jax.ShapeDtypeStruct(source.shape, f32),
         ),
-        in_specs=[anywhere] * 2,
+        in_specs=[vmem] * 2,
         out_specs=(hbm, hbm),
         scratch_shapes=[sem((1 + freqs,))],
-    )(pops, source)
+    )(
+        pltpu.with_memory_space_constraint(pops, pltpu.VMEM),
+        pltpu.with_memory_space_constraint(source, pltpu.VMEM),
+    )
 
 
 def solution(mesh):

time: 65.9 us -> 22.5 us (0.34)
  Pallas kernels: 63.4 us -> 21.7 us
  local copies, waits for them, and re-layouts: 1.69 us -> 0 us
    pallas_call x1, Pallas kernels: 42.9 us -> 1.14 us  [per_device(): pl.pallas_call(write_out, out_shape=(jax.ShapeDtypeStruct(pops.shape, f32...]
    unnamed x4 -> x0, local copies, waits for them, and re-layouts: 1.69 us -> none
where the time goes in v3:
time: 22.5 us; the launch traced here: 22.3 us
  Pallas kernels  21.7 us (96%)
  between operations  0.64 us (3%)
    pallas_call x1, Pallas kernels, per_device(): pl.pallas_call(functools.partial(kernel, (bands, tiles, slabs, depth, fre...  20.5 us
    pallas_call x1, Pallas kernels, per_device(): pl.pallas_call(write_out, out_shape=(jax.ShapeDtypeStruct(pops.shape, f32...  1.14 us

profile of v3, /device:TPU:1, one launch (start us, length us, event | category | flops | bytes accessed | tf_op | source)
XLA Modules:
  0.0 22.3 jit_solution(17820131368106681811)
XLA Ops:
  0.6 20.5 %shard_map.77 = (f32[5,8,16,64]{3,2,1,0:T(8,128)S(1)}, f32[8,8,16,256]{3,2,1,0:T(8,128)S(1)}) custom-call(f32[8]{0:T(128)} %strength_hbm.1, s32[8]{0:T(128)} %line_index_hbm.1, f32[8]{0:T(128)} %line_weight_hbm.1, f32[8,16,256]{2,1,0:T(8,128)} %opacity.1, f32[8,16,256]{2,1,0:T(8,128)} %planck.1, f32[5,8,16,256]{3,2,1,0:T(8,128)} %populations.1), custom_call_target="tpu_custom_call" | custom-call | flops 15728640 | bytes 2097152 | tf_op jit(solution)/shard_map/pallas_call | solution.py:526
  21.2 1.1 %shard_map.78 = (f32[5,8,16,64]{3,2,1,0:T(8,128)}, f32[8,8,16,256]{3,2,1,0:T(8,128)}) custom-call(f32[5,8,16,64]{3,2,1,0:T(8,128)S(1)} %get-tuple-element.4.pops, f32[8,8,16,256]{3,2,1,0:T(8,128)S(1)} %get-tuple-element.5.source), custom_call_target="tpu_custom_call" | custom-call | tf_op jit(solution)/shard_map/pallas_call | solution.py:579

commit v4 on v3

--- a/solution.py
+++ b/solution.py
@@ -137,7 +137,7 @@
         face_in[...] = jnp.zeros(face_in.shape, jnp.float32)
         face_halo[...] = jnp.zeros(face_halo.shape, jnp.float32)
 
-    acc[...] = jnp.zeros(acc.shape, jnp.float32)
+    acc[0] = jnp.zeros(acc.shape[1:], jnp.float32)
 
     def par_copies(k):
         to = {"band": lax.rem(band + k, bands)}
@@ -166,16 +166,14 @@
     lane_row = lax.broadcasted_iota(jnp.int32, (1, LANES), 1)
     indices = jnp.zeros((1, LANES), jnp.int32)
     zero = jnp.zeros((ROWS, LANES), jnp.float32)
-    rate, weight, which = zero, zero, zero
+    rate, weight = zero, zero
     for f in range(freqs):
         here = row == f
         rate = jnp.where(here, -PATH_FACTOR * strength[f], rate)
         weight = jnp.where(here, line_weight[f] * (LINES / (2.0 * freqs * bands)), weight)
-        which = jnp.where(here, line_index[f].astype(jnp.float32), which)
         indices = jnp.where(lane_row == f, line_index[f], indices)
     par_f[0, 0] = rate
     par_f[0, 1] = weight
-    par_f[0, 2] = which
     par_i[0] = indices
 
     def spread(v):
@@ -193,7 +191,8 @@
                 src[t, z, half] = EPS_THERMAL * p + (1.0 - EPS_THERMAL) * (up / (low + up))
         return carry
 
-    lax.fori_loop(0, depth, prepare, 0)
+    for z in range(depth):
+        prepare(z, 0)
 
     def layer(i, z, part):
         return opac[z, part] if i == 0 else src[i - 1, z, part]
@@ -294,7 +293,7 @@
             ),
         )
 
-    def chunk_step(k, sub):
+    def chunk_step(k, sub, latest):
         chunk = k * subs + sub
         main, to_right, to_left = face_copies(chunk)
 
@@ -310,14 +309,20 @@
         def _():
             to_left.wait_recv()
 
-        states, rates, weights, indices = [], [], [], []
+        states, rates, weights, indices, before, slots = [], [], [], [], [], []
         for f in range(BATCH):
             at = pl.ds(sub * BATCH + f, 1)
             rates.append(jnp.broadcast_to(par_f[k, 0, at], (ROWS, LANES)))
-            w = jnp.broadcast_to(par_f[k, 1, at], (ROWS, LANES))
-            t_of = jnp.broadcast_to(par_f[k, 2, at], (ROWS, LANES))
-            weights.append([jnp.where(t_of == float(t), w, 0.0) for t in range(LINES)])
-            indices.append(par_s[k, 0, sub * BATCH + f])
+            weights.append(jnp.broadcast_to(par_f[k, 1, at], (ROWS, LANES)))
+            line = par_s[k, 0, sub * BATCH + f]
+            indices.append(line)
+            slot = k * freqs + (sub * BATCH + f + 1)
+            previous = latest[0]
+            for t in range(1, LINES):
+                previous = jnp.where(line == t, latest[t], previous)
+            latest = [jnp.where(line == t, slot, latest[t]) for t in range(LINES)]
+            before.append(previous)
+            slots.append(slot)
             beyond = jnp.where(left, face_halo[0, chunk, f], face_halo[1, chunk, f])
             states.append((face_in[chunk, 0, f], face_in[chunk, 1, f], beyond))
         for z in range(depth):
@@ -342,11 +347,8 @@
                     fresh.append(out)
                 states[f] = tuple(fresh)
             for half in range(2):
-                for t in range(LINES):
-                    total = acc[t, z, half]
-                    for f in range(BATCH):
-                        total = total + weights[f][t] * states[f][half]
-                    acc[t, z, half] = total
+                for f in range(BATCH):
+                    acc[slots[f], z, half] = acc[before[f], z, half] + weights[f] * states[f][half]
         for f in range(BATCH):
             face_out[chunk, 0, f] = states[f][0]
             face_out[chunk, 1, f] = states[f][1]
@@ -363,12 +365,14 @@
         def _():
             to_left.start()
 
-    def group_step(k, carry):
+        return latest
+
+    def group_step(k, latest):
         for sub in range(subs):
-            chunk_step(k, sub)
-        return carry
-
-    lax.fori_loop(0, bands, group_step, 0)
+            latest = chunk_step(k, sub, latest)
+        return tuple(latest)
+
+    latest = lax.fori_loop(0, bands, group_step, (jnp.int32(0),) * LINES)
 
     beside = band + 1 - 2 * lax.rem(band, 2)
     across = lax.rem(band + 2, bands)
@@ -391,7 +395,7 @@
                 p = COLLISION * plk[z, half]
                 ratios = []
                 for t in range(LINES):
-                    j = acc[t, z, half]
+                    j = acc[latest[t], z, half]
                     j = j + half_turn(j)
                     ratios.append((j + p) / ((1.0 + COLLISION) + j))
                 one = 0.5 * (ratios[0] / ratios[2] + ratios[1] / ratios[3])
@@ -408,7 +412,8 @@
         gather_copy(1, band, zp, across).start()
         return carry
 
-    lax.fori_loop(0, pairs, relax, 0)
+    for zp in range(pairs):
+        relax(zp, 0)
 
     loads[6].wait()
 
@@ -537,7 +542,7 @@
             pltpu.SMEM((freqs,), f32),
             pltpu.VMEM((2 + LEVELS, depth, rows, LANES), f32),
             pltpu.VMEM((depth, rows, cells), f32),
-            pltpu.VMEM((bands, 3) + tile, f32),
+            pltpu.VMEM((bands, 2) + tile, f32),
             pltpu.VMEM((bands, 1, LANES), jnp.int32),
             pltpu.SMEM((bands, 1, LANES), jnp.int32),
             pltpu.VMEM((2, 1 + LINES, pairs // 2) + tile, f32),
@@ -548,7 +553,7 @@
             pltpu.VMEM((chunks, 2, BATCH) + tile, f32),
             pltpu.VMEM((2, chunks, BATCH) + tile, f32),
             pltpu.VMEM((chunks, 2, BATCH) + tile, f32),
-            pltpu.VMEM((LINES, depth, 2) + tile, f32),
+            pltpu.VMEM((1 + bands * freqs, depth, 2) + tile, f32),
             pltpu.VMEM((bands, pairs, 4, 2) + tile, f32),
             pltpu.VMEM((LINES, depth, rows, cells), f32),
             sem((7,)),

time: 22.5 us -> 22.6 us (level)
  no operation moved by 1% of the time
where the time goes in v4:
time: 22.6 us; the launch traced here: 22.4 us
  Pallas kernels  21.8 us (96%)
  between operations  0.64 us (3%)
    pallas_call x1, Pallas kernels, per_device(): pl.pallas_call(functools.partial(kernel, (bands, tiles, slabs, depth, fre...  20.6 us
    pallas_call x1, Pallas kernels, per_device(): pl.pallas_call(write_out, out_shape=(jax.ShapeDtypeStruct(pops.shape, f32...  1.14 us

profile of v4, /device:TPU:1, one launch (start us, length us, event | category | flops | bytes accessed | tf_op | source)
XLA Modules:
  0.0 22.4 jit_solution(7574634263061937362)
XLA Ops:
  0.6 20.6 %shard_map.77 = (f32[5,8,16,64]{3,2,1,0:T(8,128)S(1)}, f32[8,8,16,256]{3,2,1,0:T(8,128)S(1)}) custom-call(f32[8]{0:T(128)} %strength_hbm.1, s32[8]{0:T(128)} %line_index_hbm.1, f32[8]{0:T(128)} %line_weight_hbm.1, f32[8,16,256]{2,1,0:T(8,128)} %opacity.1, f32[8,16,256]{2,1,0:T(8,128)} %planck.1, f32[5,8,16,256]{3,2,1,0:T(8,128)} %populations.1), custom_call_target="tpu_custom_call" | custom-call | flops 15728640 | bytes 2097152 | tf_op jit(solution)/shard_map/pallas_call | solution.py:531
  21.3 1.1 %shard_map.78 = (f32[5,8,16,64]{3,2,1,0:T(8,128)}, f32[8,8,16,256]{3,2,1,0:T(8,128)}) custom-call(f32[5,8,16,64]{3,2,1,0:T(8,128)S(1)} %get-tuple-element.4.pops, f32[8,8,16,256]{3,2,1,0:T(8,128)S(1)} %get-tuple-element.5.source), custom_call_target="tpu_custom_call" | custom-call | tf_op jit(solution)/shard_map/pallas_call | solution.py:584

commit v5 on v4

--- a/solution.py
+++ b/solution.py
@@ -19,7 +19,7 @@
 LANES = 128
 ROWS = 8
 HALF = LANES // 2
-BATCH = 4
+BATCH = 8
 
 
 def half_turn(v):
@@ -348,7 +348,7 @@
                 states[f] = tuple(fresh)
             for half in range(2):
                 for f in range(BATCH):
-                    acc[slots[f], z, half] = acc[before[f], z, half] + weights[f] * states[f][half]
+                    acc[slots[f], z, half] = weights[f] * states[f][half]
         for f in range(BATCH):
             face_out[chunk, 0, f] = states[f][0]
             face_out[chunk, 1, f] = states[f][1]
@@ -365,6 +365,8 @@
         def _():
             to_left.start()
 
+        for f in range(BATCH):
+            acc[slots[f]] = acc[slots[f]] + acc[before[f]]
         return latest
 
     def group_step(k, latest):

time: 22.6 us -> 21.6 us (0.956)
  Pallas kernels: 21.8 us -> 20.8 us
    pallas_call x1, Pallas kernels: 20.6 us -> 19.6 us  [per_device(): pl.pallas_call(functools.partial(kernel, (bands, tiles, slabs, depth, fre...]
where the time goes in v5:
time: 21.6 us; the launch traced here: 21.4 us
  Pallas kernels  20.8 us (96%)
  between operations  0.64 us (3%)
    pallas_call x1, Pallas kernels, per_device(): pl.pallas_call(functools.partial(kernel, (bands, tiles, slabs, depth, fre...  19.6 us
    pallas_call x1, Pallas kernels, per_device(): pl.pallas_call(write_out, out_shape=(jax.ShapeDtypeStruct(pops.shape, f32...  1.14 us

profile of v5, /device:TPU:1, one launch (start us, length us, event | category | flops | bytes accessed | tf_op | source)
XLA Modules:
  0.0 21.4 jit_solution(3626125890616331501)
XLA Ops:
  0.6 19.6 %shard_map.77 = (f32[5,8,16,64]{3,2,1,0:T(8,128)S(1)}, f32[8,8,16,256]{3,2,1,0:T(8,128)S(1)}) custom-call(f32[8]{0:T(128)} %strength_hbm.1, s32[8]{0:T(128)} %line_index_hbm.1, f32[8]{0:T(128)} %line_weight_hbm.1, f32[8,16,256]{2,1,0:T(8,128)} %opacity.1, f32[8,16,256]{2,1,0:T(8,128)} %planck.1, f32[5,8,16,256]{3,2,1,0:T(8,128)} %populations.1), custom_call_target="tpu_custom_call" | custom-call | flops 15728640 | bytes 2097152 | tf_op jit(solution)/shard_map/pallas_call | solution.py:533
  20.3 1.1 %shard_map.78 = (f32[5,8,16,64]{3,2,1,0:T(8,128)}, f32[8,8,16,256]{3,2,1,0:T(8,128)}) custom-call(f32[5,8,16,64]{3,2,1,0:T(8,128)S(1)} %get-tuple-element.4.pops, f32[8,8,16,256]{3,2,1,0:T(8,128)S(1)} %get-tuple-element.5.source), custom_call_target="tpu_custom_call" | custom-call | tf_op jit(solution)/shard_map/pallas_call | solution.py:586

commit v6 on v5

--- a/solution.py
+++ b/solution.py
@@ -239,7 +239,6 @@
             copy.wait_recv()
     to_scalars = pltpu.make_async_copy(par_i, par_s, idx_sem)
     to_scalars.start()
-    to_scalars.wait()
 
     @pl.when(has_left)
     def _():
@@ -265,6 +264,8 @@
                         opac[at, 2] = v
                     else:
                         src[i - 1, at, 2] = v
+
+    to_scalars.wait()
 
     def face_copies(chunk):
         def make(part, source, target, to):
@@ -403,11 +404,6 @@
                 one = 0.5 * (ratios[0] / ratios[2] + ratios[1] / ratios[3])
                 levels = (one, ratios[1] / ratios[4], ratios[0], ratios[1])
                 both.append(levels)
-                scale = 1.0 / (1.0 + levels[0] + levels[1] + levels[2] + levels[3])
-                rows = pl.ds(half * ROWS, ROWS)
-                pops_out[0, z, rows] = scale[:, :HALF]
-                for i in range(4):
-                    pops_out[1 + i, z, rows] = (scale * levels[i])[:, :HALF]
             for i in range(4):
                 gathered[band, zp, i, half] = jnp.where(left, both[0][i], both[1][i])
         gather_copy(0, band, zp, beside).start()
@@ -427,6 +423,18 @@
         return carry
 
     lax.fori_loop(0, pairs // 2, forward, 0)
+
+    def normalise(zp, carry):
+        for half in range(2):
+            rows = pl.ds(half * ROWS, ROWS)
+            levels = [gathered[band, zp, i, half] for i in range(4)]
+            scale = 1.0 / (1.0 + levels[0] + levels[1] + levels[2] + levels[3])
+            for i, v in enumerate([scale] + [scale * level for level in levels]):
+                pops_out[i, zp, rows] = v[:, :HALF]
+                pops_out[i, zp + pairs, rows] = half_turn(v)[:, :HALF]
+        return carry
+
+    lax.fori_loop(0, pairs, normalise, 0)
 
     def finish_two(q, carry):
         gather_copy(1, across, 2 * q, across).wait_recv()

time: 21.6 us -> 21.5 us (level)
  no operation moved by 1% of the time
where the time goes in v6:
time: 21.5 us; the launch traced here: 21.4 us
  Pallas kernels  20.7 us (96%)
  between operations  0.64 us (3%)
    pallas_call x1, Pallas kernels, per_device(): pl.pallas_call(functools.partial(kernel, (bands, tiles, slabs, depth, fre...  19.6 us
    pallas_call x1, Pallas kernels, per_device(): pl.pallas_call(write_out, out_shape=(jax.ShapeDtypeStruct(pops.shape, f32...  1.14 us

profile of v6, /device:TPU:1, one launch (start us, length us, event | category | flops | bytes accessed | tf_op | source)
XLA Modules:
  0.0 21.4 jit_solution(16087618013251639297)
XLA Ops:
  0.6 19.6 %shard_map.77 = (f32[5,8,16,64]{3,2,1,0:T(8,128)S(1)}, f32[8,8,16,256]{3,2,1,0:T(8,128)S(1)}) custom-call(f32[8]{0:T(128)} %strength_hbm.1, s32[8]{0:T(128)} %line_index_hbm.1, f32[8]{0:T(128)} %line_weight_hbm.1, f32[8,16,256]{2,1,0:T(8,128)} %opacity.1, f32[8,16,256]{2,1,0:T(8,128)} %planck.1, f32[5,8,16,256]{3,2,1,0:T(8,128)} %populations.1), custom_call_target="tpu_custom_call" | custom-call | flops 15728640 | bytes 2097152 | tf_op jit(solution)/shard_map/pallas_call | solution.py:541
  20.2 1.1 %shard_map.78 = (f32[5,8,16,64]{3,2,1,0:T(8,128)}, f32[8,8,16,256]{3,2,1,0:T(8,128)}) custom-call(f32[5,8,16,64]{3,2,1,0:T(8,128)S(1)} %get-tuple-element.4.pops, f32[8,8,16,256]{3,2,1,0:T(8,128)S(1)} %get-tuple-element.5.source), custom_call_target="tpu_custom_call" | custom-call | tf_op jit(solution)/shard_map/pallas_call | solution.py:594

commit v7 on v6

--- a/solution.py
+++ b/solution.py
@@ -408,21 +408,13 @@
                 gathered[band, zp, i, half] = jnp.where(left, both[0][i], both[1][i])
         gather_copy(0, band, zp, beside).start()
         gather_copy(1, band, zp, across).start()
+        gather_copy(2, band, zp, corner).start()
         return carry
 
     for zp in range(pairs):
         relax(zp, 0)
 
     loads[6].wait()
-
-    def forward(q, carry):
-        gather_copy(0, beside, 2 * q, beside).wait_recv()
-        gather_copy(2, beside, 2 * q, across).start()
-        gather_copy(1, across, 2 * q + 1, across).wait_recv()
-        gather_copy(2, across, 2 * q + 1, beside).start()
-        return carry
-
-    lax.fori_loop(0, pairs // 2, forward, 0)
 
     def normalise(zp, carry):
         for half in range(2):
@@ -437,10 +429,12 @@
     lax.fori_loop(0, pairs, normalise, 0)
 
     def finish_two(q, carry):
+        gather_copy(0, beside, 2 * q, beside).wait_recv()
         gather_copy(1, across, 2 * q, across).wait_recv()
         gather_copy(2, corner, 2 * q, corner).wait_recv()
         finish(2 * q)
         gather_copy(0, beside, 2 * q + 1, beside).wait_recv()
+        gather_copy(1, across, 2 * q + 1, across).wait_recv()
         gather_copy(2, corner, 2 * q + 1, corner).wait_recv()
         finish(2 * q + 1)
         return carry
@@ -510,7 +504,7 @@
     def drain_gather(zp, carry):
         gather_copy(0, band, zp, beside).wait_send()
         gather_copy(1, band, zp, across).wait_send()
-        gather_copy(2, corner, zp, across).wait_send()
+        gather_copy(2, band, zp, corner).wait_send()
         return carry
 
     lax.fori_loop(0, pairs, drain_gather, 0)

time: 21.5 us -> 21 us (0.977)
  Pallas kernels: 20.7 us -> 20.2 us
    pallas_call x1, Pallas kernels: 19.6 us -> 19.1 us  [per_device(): pl.pallas_call(functools.partial(kernel, (bands, tiles, slabs, depth, fre...]
where the time goes in v7:
time: 21 us; the launch traced here: 20.9 us
  Pallas kernels  20.2 us (96%)
  between operations  0.64 us (3%)
    pallas_call x1, Pallas kernels, per_device(): pl.pallas_call(functools.partial(kernel, (bands, tiles, slabs, depth, fre...  19.1 us
    pallas_call x1, Pallas kernels, per_device(): pl.pallas_call(write_out, out_shape=(jax.ShapeDtypeStruct(pops.shape, f32...  1.14 us

profile of v7, /device:TPU:1, one launch (start us, length us, event | category | flops | bytes accessed | tf_op | source)
XLA Modules:
  0.0 20.9 jit_solution(9853402337431996252)
XLA Ops:
  0.6 19.1 %shard_map.77 = (f32[5,8,16,64]{3,2,1,0:T(8,128)S(1)}, f32[8,8,16,256]{3,2,1,0:T(8,128)S(1)}) custom-call(f32[8]{0:T(128)} %strength_hbm.1, s32[8]{0:T(128)} %line_index_hbm.1, f32[8]{0:T(128)} %line_weight_hbm.1, f32[8,16,256]{2,1,0:T(8,128)} %opacity.1, f32[8,16,256]{2,1,0:T(8,128)} %planck.1, f32[5,8,16,256]{3,2,1,0:T(8,128)} %populations.1), custom_call_target="tpu_custom_call" | custom-call | flops 15728640 | bytes 2097152 | tf_op jit(solution)/shard_map/pallas_call | solution.py:535
  19.7 1.1 %shard_map.78 = (f32[5,8,16,64]{3,2,1,0:T(8,128)}, f32[8,8,16,256]{3,2,1,0:T(8,128)}) custom-call(f32[5,8,16,64]{3,2,1,0:T(8,128)S(1)} %get-tuple-element.4.pops, f32[8,8,16,256]{3,2,1,0:T(8,128)S(1)} %get-tuple-element.5.source), custom_call_target="tpu_custom_call" | custom-call | tf_op jit(solution)/shard_map/pallas_call | solution.py:588

commit v8 on v7

--- a/solution.py
+++ b/solution.py
@@ -354,17 +354,17 @@
             face_out[chunk, 0, f] = states[f][0]
             face_out[chunk, 1, f] = states[f][1]
 
+        @pl.when(has_down & has_right)
+        def _():
+            to_right.start()
+
+        @pl.when(has_down & has_left)
+        def _():
+            to_left.start()
+
         @pl.when(has_down)
         def _():
             main.start()
-
-        @pl.when(has_down & has_right)
-        def _():
-            to_right.start()
-
-        @pl.when(has_down & has_left)
-        def _():
-            to_left.start()
 
         for f in range(BATCH):
             acc[slots[f]] = acc[slots[f]] + acc[before[f]]
@@ -406,9 +406,9 @@
                 both.append(levels)
             for i in range(4):
                 gathered[band, zp, i, half] = jnp.where(left, both[0][i], both[1][i])
+        gather_copy(2, band, zp, corner).start()
         gather_copy(0, band, zp, beside).start()
         gather_copy(1, band, zp, across).start()
-        gather_copy(2, band, zp, corner).start()
         return carry
 
     for zp in range(pairs):

time: 21 us -> 20.7 us (0.986)
  Pallas kernels: 20.2 us -> 19.9 us
    pallas_call x1, Pallas kernels: 19.1 us -> 18.7 us  [per_device(): pl.pallas_call(functools.partial(kernel, (bands, tiles, slabs, depth, fre...]
where the time goes in v8:
time: 20.7 us; the launch traced here: 20.5 us
  Pallas kernels  19.9 us (96%)
  between operations  0.64 us (3%)
    pallas_call x1, Pallas kernels, per_device(): pl.pallas_call(functools.partial(kernel, (bands, tiles, slabs, depth, fre...  18.7 us
    pallas_call x1, Pallas kernels, per_device(): pl.pallas_call(write_out, out_shape=(jax.ShapeDtypeStruct(pops.shape, f32...  1.14 us

profile of v8, /device:TPU:1, one launch (start us, length us, event | category | flops | bytes accessed | tf_op | source)
XLA Modules:
  0.0 20.5 jit_solution(9301432737982585059)
XLA Ops:
  0.6 18.7 %shard_map.77 = (f32[5,8,16,64]{3,2,1,0:T(8,128)S(1)}, f32[8,8,16,256]{3,2,1,0:T(8,128)S(1)}) custom-call(f32[8]{0:T(128)} %strength_hbm.1, s32[8]{0:T(128)} %line_index_hbm.1, f32[8]{0:T(128)} %line_weight_hbm.1, f32[8,16,256]{2,1,0:T(8,128)} %opacity.1, f32[8,16,256]{2,1,0:T(8,128)} %planck.1, f32[5,8,16,256]{3,2,1,0:T(8,128)} %populations.1), custom_call_target="tpu_custom_call" | custom-call | flops 15728640 | bytes 2097152 | tf_op jit(solution)/shard_map/pallas_call | solution.py:535
  19.4 1.1 %shard_map.78 = (f32[5,8,16,64]{3,2,1,0:T(8,128)}, f32[8,8,16,256]{3,2,1,0:T(8,128)}) custom-call(f32[5,8,16,64]{3,2,1,0:T(8,128)S(1)} %get-tuple-element.4.pops, f32[8,8,16,256]{3,2,1,0:T(8,128)S(1)} %get-tuple-element.5.source), custom_call_target="tpu_custom_call" | custom-call | tf_op jit(solution)/shard_map/pallas_call | solution.py:588
